TPU v7x, 256 devices: a whole 4x4x8 slice. The times are simulated.
256 devices in a mesh: group: 16 (over z, x_hi), dp: 16 (over x_lo, y, core).
Axes of the slice: x: 4 (x_hi: 2, x_lo: 2; x = x_hi * 2 + x_lo), y: 4, z: 8, core: 2. Of those that a mesh axis runs over, the one named last changes fastest.
Arguments:
- img_feat: bfloat16 [16, 4096, 1152], P('group', 'dp'), may hold values from -6 to 6
- txt_feat: bfloat16 [16, 4096, 1152], P('group', 'dp'), may hold values from -6 to 6
- group_weights: bfloat16 [16, 2, 1152, 1152], P('group', None, 'dp'), may hold values from -0.1875 to 0.1875
- drift: bfloat16 [16, 2, 1152, 1152], P('group', None, 'dp'), may hold values from -3 to 3
- logit_params: float32 [2], replicated, may hold values from -2 to 3, as said below
Outputs:
- outer_step: float32 [2, 1152, 1152], P(None, 'dp')
Inputs may be any that keep to these rules, and one draw needn't show every extreme that they name: logit_params[0] lies in 2 to 3 and logit_params[1] in -2 to 0.
All inputs are finite; a program needn't handle non-finite values.
Results may differ from a plain program's by a relative error of at most 0.012.
Values may be sent and summed in bfloat16 or wider, within the bound.
No kernel may reach another device: no remote copies, remote signals or barrier semaphores. Data moves between devices by JAX's collectives and lax.ppermute only.
A program may use at most 128 MiB of HBM per device.

v0:
```python
import jax
import jax.numpy as jnp
from jax import lax
from jax.sharding import PartitionSpec as P


def finish_norm(raw):
    nrm = jnp.sqrt(jnp.sum(raw * raw, axis=1, keepdims=True) + 1e-06)
    return (raw / nrm, nrm)


def back_norm(unit, nrm, dz):
    return ((dz - unit * jnp.sum(unit * dz, axis=1, keepdims=True)) / nrm).astype(jnp.bfloat16)


def derivative(score, label):
    return (-label * jax.nn.sigmoid(-label * score)).astype(jnp.bfloat16)


def local(img_feat, txt_feat, group_weights, drift, logit_params):
    x_img = img_feat[0]
    x_txt = txt_feat[0]
    rows = x_img.shape[0]
    width = group_weights.shape[3]
    scale = jnp.exp(logit_params[0])
    bias = logit_params[1]
    mine = lax.axis_index("dp") * rows
    piece = lax.all_gather(group_weights, "dp", axis=2, tiled=True)
    left_img = x_img
    left_txt = x_txt
    u_img = jnp.dot(left_img, piece[0, 0], preferred_element_type=jnp.float32)
    u_txt = jnp.dot(left_txt, piece[0, 1], preferred_element_type=jnp.float32)
    zf_img, n_img = finish_norm(u_img)
    zf_txt, n_txt = finish_norm(u_txt)
    z_img = zf_img.astype(jnp.bfloat16)
    z_txt = zf_txt.astype(jnp.bfloat16)
    piece = lax.all_gather(z_txt, "dp", axis=0, tiled=True)
    score = scale * jnp.einsum("ie,je->ij", z_img, piece, preferred_element_type=jnp.float32) + bias
    own = mine + lax.broadcasted_iota(jnp.int32, score.shape, 0)
    other = lax.broadcasted_iota(jnp.int32, score.shape, 1)
    label = jnp.where(own == other, 1.0, -1.0).astype(jnp.float32)
    block = derivative(score, label)
    dz = scale * jnp.dot(block, piece, preferred_element_type=jnp.float32)
    text_table = block
    block = text_table
    dz_txt = lax.psum_scatter(
        (scale * jnp.einsum("ij,ie->je", block, z_img, preferred_element_type=jnp.float32)).astype(
            jnp.bfloat16
        ),
        "dp",
        scatter_dimension=0,
        tiled=True,
    ).astype(jnp.float32)
    du_img = back_norm(zf_img, n_img, dz)
    du_txt = back_norm(zf_txt, n_txt, dz_txt)
    left_img = x_img
    left_txt = x_txt
    grad_img = jnp.einsum("ik,ie->ke", left_img, du_img, preferred_element_type=jnp.float32)
    grad_txt = jnp.einsum("ik,ie->ke", left_txt, du_txt, preferred_element_type=jnp.float32)
    summed = lax.psum_scatter(
        jnp.concatenate([grad_img, grad_txt], axis=1), "dp", scatter_dimension=0, tiled=True
    )
    grads = jnp.stack([summed[:, :width], summed[:, width:]])
    pseudo = drift[0].astype(jnp.float32) + grads
    outer = lax.psum(pseudo, "group")
    return outer / lax.axis_size("group")


def solution(mesh):
    return jax.shard_map(
        local,
        mesh=mesh,
        in_specs=(
            P("group", "dp", None),
            P("group", "dp", None),
            P("group", None, "dp", None),
            P("group", None, "dp", None),
            P(),
        ),
        out_specs=P(None, "dp", None),
        check_vma=False,
    )
```

profile of v0, /device:TPU:8, one launch (start us, length us, event | category | flops | bytes accessed | tf_op | source)
XLA Modules:
  0.0 489.9 jit_solution(15382276007341674140)
XLA Ops:
  6.5 0.7 all-gather.3.cloned.1.call-update
  7.3 0.0 all-gather.5.cloned.1.call-start
  7.3 46.4 %all-gather.3.cloned.1.call-done = bf16[1,2,1152,1152]{3,2,1,0:T(8,128)(2,1)} async-done(((bf16[1,2,72,1152]{3,2,1,0:T(8,128)(2,1)}), bf16[1,2,1152,1152]{3,2,1,0:T(8,128)(2,1)}) %all-gather.3.cloned.1.call-update) | async-done | bytes 5308432 | tf_op jit(solution)/shard_map/all_gather | solution.py:28
  53.7 3.0 multiply_reduce_fusion.1
  56.7 0.0 copy-start.3
  56.7 1.0 fusion.25
  57.7 0.0 all-gather.5.cloned.1.call-update
  57.7 0.0 reduce-scatter.5.cloned.1.call-start
  57.8 0.7 fusion.26
  59.1 2.8 multiply_reduce_fusion.2
  61.9 55.9 %all-gather.5.cloned.1.call-done = bf16[4096,1152]{1,0:T(8,128)(2,1)} async-done(((bf16[256,1152]{1,0:T(8,128)(2,1)}), bf16[4096,1152]{1,0:T(8,128)(2,1)}) %all-gather.5.cloned.1.call-update) | async-done | bytes 9437200 | tf_op jit(solution)/shard_map/all_gather | solution.py:37
  117.8 8.1 %fusion.8 = bf16[256,4096]{1,0:T(8,128)(2,1)S(1)} fusion(bf16[4096,1152]{1,0:T(8,128)(2,1)} %all-gather.5.cloned.1.call-done, f32[]{:T(128)} %bitcast.6, f32[]{:T(128)} %bitcast.1, s32[256]{0:T(256)S(1)} %iota_add_fusion, f32[256,1152]{1,0:T(8,128)S(1)} %get-tuple-element.12, f32[256]{0:T(256)S(1)} %add_sqrt_fusion.1), kind=kOutput, calls=%fused_computation.13 | convolution fusion | flops 2428043264 | bytes 12716040 | tf_op jit(solution)/shard_map/ie,je->ij/dot_general | solution.py:38
  125.9 1.3 copy-done.5
  127.2 5.4 %fusion = bf16[4096,1152]{1,0:T(8,128)(2,1)} fusion(bf16[256,4096]{1,0:T(8,128)(2,1)S(1)} %fusion.8, f32[]{:T(128)} %bitcast.1, f32[256,1152]{1,0:T(8,128)S(1)} %get-tuple-element.12, f32[256]{0:T(256)S(1)} %add_sqrt_fusion.1), kind=kOutput, calls=%fused_computation.1 | convolution fusion | flops 2425946112 | bytes 12715012 | tf_op jit(solution)/shard_map/ij,ie->je/dot_general | solution.py:47
  132.6 0.0 reduce-scatter.5.cloned.1.call-update
  132.6 0.2 reduce-scatter.7.cloned.1.call-start
  132.9 7.3 %multiply_reduce_fusion = (f32[256]{0:T(256)S(1)}, f32[256,1152]{1,0:T(8,128)S(1)}) fusion(f32[256,1152]{1,0:T(8,128)S(1)} %get-tuple-element.12, f32[256]{0:T(256)S(1)} %add_sqrt_fusion.1, bf16[256,4096]{1,0:T(8,128)(2,1)} %copy-done.5, bf16[4096,1152]{1,0:T(8,128)(2,1)} %all-gather.5.cloned.1.call-done, f32[]{:T(128)} %bitcast.1), kind=kOutput, calls=%fused_computation.26 | convolution fusion | flops 2417098496 | bytes 13895684 | tf_op jit(solution)/shard_map/dot_general | solution.py:43
  140.2 0.0 copy-start.4
  140.2 3.5 convolution_bitcast_fusion.1
  143.7 64.8 %reduce-scatter.5.cloned.1.call-done = bf16[256,1152]{1,0:T(8,128)(2,1)} async-done(((bf16[4096,1152]{1,0:T(8,128)(2,1)}), bf16[256,1152]{1,0:T(8,128)(2,1)}) %reduce-scatter.5.cloned.1.call-update) | async-done | bytes 589840 | tf_op jit(solution)/shard_map/reduce_scatter | solution.py:46
  208.5 1.4 fusion.11
  209.9 4.6 convolution_bitcast_fusion
  214.5 8.8 %pad_maximum_fusion = f32[1152,2304]{0,1:T(8,128)} fusion(f32[1152,1152]{0,1:T(8,128)} %convolution_bitcast_fusion, f32[1152,1152]{0,1:T(8,128)} %convolution_bitcast_fusion.1), kind=kLoop, calls=%fused_computation.2 | loop fusion | flops 2654208 | bytes 21233664 | tf_op jit(solution)/shard_map/concatenate | solution.py:61
  223.3 12.7 %copy.12 = f32[1152,2304]{1,0:T(8,128)} copy(f32[1152,2304]{0,1:T(8,128)} %pad_maximum_fusion) | data formatting | bytes 21233664
  235.9 0.0 reduce-scatter.7.cloned.1.call-update
  236.0 0.0 all-reduce.2.cloned.1.call-start
  236.0 79.7 %reduce-scatter.7.cloned.1.call-done = f32[72,2304]{1,0:T(8,128)} async-done(((f32[1152,2304]{1,0:T(8,128)}), f32[72,2304]{1,0:T(8,128)}) %reduce-scatter.7.cloned.1.call-update) | async-done | bytes 663568 | tf_op jit(solution)/shard_map/reduce_scatter | solution.py:60
  315.7 1.2 slice_bitcast_fusion.5
  316.9 0.9 maximum_add_fusion
  317.8 0.0 all-reduce.2.cloned.1.call-update
  317.8 163.6 %all-reduce.2.cloned.1.call-done = f32[2,72,1152]{2,1,0:T(8,128)} async-done(((f32[2,72,1152]{2,1,0:T(8,128)}), f32[2,72,1152]{2,1,0:T(8,128)}) %all-reduce.2.cloned.1.call-update) | async-done | bytes 663568 | tf_op jit(solution)/shard_map/psum | solution.py:65
  481.4 2.0 broadcast_multiply_fusion
  (13 shorter events, 0.0 us)
Async XLA Ops:
  6.5 52.5 %copy-start = (bf16[1,256,1152]{2,1,0:T(8,128)(2,1)S(1)}, bf16[1,256,1152]{2,1,0:T(8,128)(2,1)}, u32[]{:S(2)}) copy-start(bf16[1,256,1152]{2,1,0:T(8,128)(2,1)} %param.5) | copy-start | bytes 1769476
  6.5 47.2 %all-gather.3.cloned.1.call-start = ((), (), s32[]{:S(2)}) async-start(), calls=%async_computation.2 | async-start | bytes 5640192 | tf_op jit(solution)/shard_map/all_gather | solution.py:28
  7.3 110.5 %all-gather.5.cloned.1.call-start = ((), (), s32[]{:S(2)}) async-start(), calls=%async_computation.3 | async-start | bytes 10027008 | tf_op jit(solution)/shard_map/all_gather | solution.py:37
  56.7 1.1 copy-start.3
  57.7 150.8 %reduce-scatter.5.cloned.1.call-start = ((), (), s32[]{:S(2)}) async-start(), calls=%async_computation.4 | async-start | bytes 10027008 | tf_op jit(solution)/shard_map/reduce_scatter | solution.py:46
  125.9 1.3 copy-start.5
  132.6 183.0 %reduce-scatter.7.cloned.1.call-start = ((), (), s32[]{:S(2)}) async-start(), calls=%async_computation.6 | async-start | bytes 11280384 | tf_op jit(solution)/shard_map/reduce_scatter | solution.py:60
  140.2 69.7 %copy-start.4 = (bf16[1,256,1152]{2,1,0:T(8,128)(2,1)S(1)}, bf16[1,256,1152]{2,1,0:T(8,128)(2,1)}, u32[]{:S(2)}) copy-start(bf16[1,256,1152]{2,1,0:T(8,128)(2,1)} %param.6) | copy-start | bytes 1769476
  235.9 80.9 %copy-start.2 = (bf16[1,2,72,1152]{3,2,1,0:T(8,128)(2,1)S(1)}, bf16[1,2,72,1152]{3,2,1,0:T(8,128)(2,1)}, u32[]{:S(2)}) copy-start(bf16[1,2,72,1152]{3,2,1,0:T(8,128)(2,1)} %param.8) | copy-start | bytes 995332
  236.0 245.5 %all-reduce.2.cloned.1.call-start = ((), (), s32[]{:S(2)}) async-start(), calls=%async_computation.5 | async-start | bytes 1327104 | tf_op jit(solution)/shard_map/psum | solution.py:65
  315.7 167.7 %copy-start.1 = (bf16[1,256,1152]{2,1,0:T(8,128)(2,1)S(1)}, bf16[1,256,1152]{2,1,0:T(8,128)(2,1)}, u32[]{:S(2)}) copy-start(bf16[1,256,1152]{2,1,0:T(8,128)(2,1)} %param.5) | copy-start | bytes 1769476
Sparse Core Ops, SparseCore 0:
  9.2 44.4 all-gather.2
  57.8 59.8 all-gather.4
  132.8 75.6 reduce-scatter.4
  236.1 79.5 reduce-scatter.6
  318.2 163.2 all-reduce.1
where the time goes:
time: 491 us; the launch traced here: 490 us
  waiting for transfers between devices  411 us (84%)
  matrix products  34.8 us (7%)
  local copies, waits for them, and re-layouts  15.8 us (3%)
  other arithmetic  14 us (3%)
  between operations  13.8 us (3%)
    psum x1, waiting for transfers between devices, local(): outer = lax.psum(pseudo, 'group')  164 us
    reduce_scatter x1, waiting for transfers between devices, local(): lax.psum_scatter(jnp.concatenate([grad_img, grad_txt], axis=1), 'dp', sca...  79.7 us
    reduce_scatter x1, waiting for transfers between devices, local(): lax.psum_scatter((scale * jnp.einsum('ij,ie->je', block, z_img, preferred...  64.8 us
    all_gather x1, waiting for transfers between devices, local(): piece = lax.all_gather(z_txt, 'dp', axis=0, tiled=True)  55.9 us
    all_gather x1, waiting for transfers between devices, local(): piece = lax.all_gather(group_weights, 'dp', axis=2, tiled=True)  46.4 us
    unnamed x13, local copies, waits for them, and re-layouts  14 us
  transfers between devices with their start and end apart: 5, of which 5 were waited for; matrix products, arithmetic and copies ran while one was open for 3% of the time, Pallas kernels for 0%

commit v1 on v0

v1 whole, which is shorter than its diff:
```python
import jax
import jax.numpy as jnp
from jax import lax
from jax.sharding import Mesh, PartitionSpec as P

BF = jnp.bfloat16
F32 = jnp.float32
CHIPS = ("xl", "y")
GROUP = ("z", "xh")


def shift_y(x, by):
    return lax.ppermute(x, "y", [(i, (i + by) % 4) for i in range(4)])


def swap_x(x):
    return lax.ppermute(x, "xl", [(0, 1), (1, 0)])


def swap_core(x):
    return lax.ppermute(x, "c", [(0, 1), (1, 0)])


def exchange(x, axes):
    return lax.all_to_all(x, axes, split_axis=0, concat_axis=0, tiled=True)


def dot(a, b, dims):
    return lax.dot_general(a, b, (dims, ((), ())), preferred_element_type=F32)


def embed(x, w):
    u = dot(x, w, ((1,), (0,)))
    nrm = jnp.sqrt(jnp.sum(u * u, axis=1, keepdims=True) + 1e-06)
    return u / nrm, nrm


def back_norm(unit, nrm, dz):
    return ((dz - unit * jnp.sum(unit * dz, axis=1, keepdims=True)) / nrm).astype(BF)


def local(img_feat, txt_feat, group_weights, drift, logit_params):
    core = lax.axis_index("c")
    first = core == 0
    x_img, x_txt = img_feat[0], txt_feat[0]
    rows = x_img.shape[0]
    scale = jnp.exp(logit_params[0])
    bias = logit_params[1]

    weights = lax.all_gather(group_weights[0], ("xl", "y", "c"), axis=1, tiled=True)
    txt_x = swap_x(x_txt)
    x_img = jnp.concatenate([x_img, shift_y(x_img, 1), shift_y(x_img, 3), shift_y(x_img, 2)], 0)
    x_txt = jnp.concatenate([x_txt, swap_core(x_txt), txt_x, swap_core(txt_x)], 0)
    kept, given = jnp.where(first, drift[0, 0], drift[0, 1]), jnp.where(first, drift[0, 1], drift[0, 0])
    got = swap_core(given)
    shift = jnp.concatenate([jnp.where(first, kept, got), jnp.where(first, got, kept)], 0)

    zf_img, n_img = embed(x_img, weights[0])
    zf_txt, n_txt = embed(x_txt, weights[1])
    z_img, z_txt = zf_img.astype(BF), zf_txt.astype(BF)
    score = scale * dot(z_img, z_txt, ((1,), (1,))) + bias
    i = lax.broadcasted_iota(jnp.int32, score.shape, 0)
    j = lax.broadcasted_iota(jnp.int32, score.shape, 1)
    label = jnp.where((i == j) & (i < rows), 1.0, -1.0).astype(F32)
    gb = (-label * jax.nn.sigmoid(-label * score)).astype(BF)
    du_img = back_norm(zf_img, n_img, scale * dot(gb, z_txt, ((1,), (0,))))
    du_txt = back_norm(zf_txt, n_txt, scale * dot(gb, z_img, ((0,), (0,))))
    g_img = dot(x_img, du_img, ((0,), (0,))).astype(BF)
    g_txt = dot(x_txt, du_txt, ((0,), (0,))).astype(BF)

    mine = jnp.where(first, g_img, g_txt).astype(F32) + swap_core(jnp.where(first, g_txt, g_img)).astype(F32)
    d, e = mine.shape
    parts = exchange(mine.astype(BF).reshape(8, d // 8, e), CHIPS)
    block = jnp.sum(parts.astype(F32), axis=0) + shift.astype(F32)
    h = d // 8
    tiles = block.reshape(h // 8, 8, e // 128, 128).transpose(0, 2, 1, 3).reshape(-1, 8, 128)
    n = tiles.shape[0]
    each = -(-n // 16)
    tiles = jnp.pad(tiles, ((0, 16 * each - n), (0, 0), (0, 0))).reshape(16, each * 8, 128)
    total = jnp.sum(exchange(tiles.astype(BF), GROUP).astype(F32), axis=0) * (1.0 / 16)
    out = exchange(jnp.broadcast_to(total[None], (16, each * 8, 128)), GROUP)
    out = out.reshape(16 * each, 8, 128)[:n].reshape(h // 8, e // 128, 8, 128).transpose(0, 2, 1, 3)
    out = out.reshape(2, h // 2, e)
    keep = jnp.where(first, out[0], out[1])
    other = swap_core(jnp.where(first, out[1], out[0]))
    return jnp.stack([jnp.where(first, keep, other), jnp.where(first, other, keep)])


def solution(mesh):
    fine = Mesh(mesh.devices.reshape(8, 2, 2, 4, 2), ("z", "xh", "xl", "y", "c"))
    dp = ("xl", "y", "c")
    return jax.shard_map(
        local,
        mesh=fine,
        in_specs=(
            P(GROUP, dp, None),
            P(GROUP, dp, None),
            P(GROUP, None, dp, None),
            P(GROUP, None, dp, None),
            P(),
        ),
        out_specs=P(None, dp, None),
        check_vma=False,
    )
```

time: 491 us -> 203 us (0.41)
  waiting for transfers between devices: 411 us -> 87.5 us
  blocking collectives: 0 us -> 50.3 us
  local copies, waits for them, and re-layouts: 15.8 us -> 1.47 us
  starting transfers between devices: 0.35 us -> 11.7 us
  other arithmetic: 14 us -> 4.13 us
  matrix products: 34.8 us -> 29.8 us
    psum x1 -> x0, waiting for transfers between devices: 164 us -> none  [local(): outer = lax.psum(pseudo, 'group')]
    reduce_scatter x2 -> x0, waiting for transfers between devices: 144 us -> none  [the longest x1 79.7 us: local(): lax.psum_scatter(jnp.concatenate([grad_img, grad_txt], axis=1), 'dp', sca...]
    all_gather x2 -> x1, waiting for transfers between devices: 102 us -> 11.7 us  [local(): lax.all_gather(group_weights[0], ('xl', 'y', 'c'), axis=1, tiled=True)]
    all_to_all x0 -> x2, blocking collectives: none -> 50.3 us  [exchange(): return lax.all_to_all(x, axes, split_axis=0, concat_axis=0, tiled=True)]
    ppermute x0 -> x9, waiting for transfers between devices: none -> 45.4 us  [the longest x3 30.3 us: shift_y(): return lax.ppermute(x, 'y', [(i, (i + by) % 4) for i in range(4)])]
    all_to_all x0 -> x1, waiting for transfers between devices: none -> 29.7 us  [exchange(): return lax.all_to_all(x, axes, split_axis=0, concat_axis=0, tiled=True)]
    unnamed x13 -> x8, local copies, waits for them, and re-layouts: 14 us -> 0.02 us
    concatenate x1 -> x0, other arithmetic: 8.79 us -> none  [local(): jnp.concatenate([grad_img, grad_txt], axis=1)]
  transfers between devices with their start and end apart: 5 -> 11, of which waited for: 5 -> 9; matrix products, arithmetic and copies ran while one was open for 3% -> 4% of each run, Pallas kernels for 0% -> 0%
where the time goes in v1:
time: 203 us; the launch traced here: 199 us
  waiting for transfers between devices  87.5 us (43%)
  blocking collectives  50.3 us (25%)
  matrix products  29.8 us (15%)
  between operations  14.3 us (7%)
  starting transfers between devices  11.7 us (6%)
  other arithmetic  4.13 us (2%)
    all_to_all x2, blocking collectives, exchange(): return lax.all_to_all(x, axes, split_axis=0, concat_axis=0, tiled=True)  50.3 us
    ppermute x3, waiting for transfers between devices, shift_y(): return lax.ppermute(x, 'y', [(i, (i + by) % 4) for i in range(4)])  30.3 us
    dot_general x7, matrix products, dot(): return lax.dot_general(a, b, (dims, ((), ())), preferred_element_type=F32)  29.8 us
    all_to_all x1, waiting for transfers between devices, exchange(): return lax.all_to_all(x, axes, split_axis=0, concat_axis=0, tiled=True)  29.7 us
    all_gather x1, waiting for transfers between devices, local(): lax.all_gather(group_weights[0], ('xl', 'y', 'c'), axis=1, tiled=True)  11.7 us
    ppermute x5, waiting for transfers between devices, swap_core(): return lax.ppermute(x, 'c', [(0, 1), (1, 0)])  7.74 us
    ppermute x1, waiting for transfers between devices, swap_x(): return lax.ppermute(x, 'xl', [(0, 1), (1, 0)])  7.4 us
    all_to_all x1, starting transfers between devices, exchange(): return lax.all_to_all(x, axes, split_axis=0, concat_axis=0, tiled=True)  5.28 us
  transfers between devices with their start and end apart: 11, of which 9 were waited for; matrix products, arithmetic and copies ran while one was open for 4% of the time, Pallas kernels for 0%

profile of v1, /device:TPU:8, one launch (start us, length us, event | category | flops | bytes accessed | tf_op | source)
XLA Modules:
  0.0 199.2 jit_solution(290466484669314458)
XLA Ops:
  6.5 0.7 all-gather.3.cloned.1.call-update
  7.3 1.6 collective-permute-start.4
  8.8 2.3 %collective-permute-start.2 = (bf16[256,1152]{1,0:T(8,128)(2,1)}, bf16[256,1152]{1,0:T(8,128)(2,1)S(1)}, u32[]{:S(2)}, u32[]{:S(2)}) collective-permute-start(bf16[256,1152]{1,0:T(8,128)(2,1)} %bitcast.51), channel_id=1, source_target_pairs={{0,4},{2,6},{4,0},{6,2},{1,5},{3,7},{5,1},{7,3},{8,12},{10,14},{12... | collective-permute-start | bytes 1769480 | tf_op jit(solution)/shard_map/ppermute | solution.py:13
  11.1 1.3 collective-permute-start.1
  12.5 0.7 collective-permute-start
  13.2 1.3 fusion.17
  15.2 7.4 %collective-permute-done.4 = bf16[256,1152]{1,0:T(8,128)(2,1)S(1)} collective-permute-done((bf16[256,1152]{1,0:T(8,128)(2,1)}, bf16[256,1152]{1,0:T(8,128)(2,1)S(1)}, u32[]{:S(2)}, u32[]{:S(2)}) %collective-permute-start.4) | collective-permute-done | bytes 589856 | tf_op jit(solution)/shard_map/ppermute | solution.py:17
  22.6 4.6 %collective-permute-done.2 = bf16[256,1152]{1,0:T(8,128)(2,1)S(1)} collective-permute-done((bf16[256,1152]{1,0:T(8,128)(2,1)}, bf16[256,1152]{1,0:T(8,128)(2,1)S(1)}, u32[]{:S(2)}, u32[]{:S(2)}) %collective-permute-start.2) | collective-permute-done | bytes 589856 | tf_op jit(solution)/shard_map/ppermute | solution.py:13
  27.2 23.1 %collective-permute-done.1 = bf16[256,1152]{1,0:T(8,128)(2,1)S(1)} collective-permute-done((bf16[256,1152]{1,0:T(8,128)(2,1)}, bf16[256,1152]{1,0:T(8,128)(2,1)S(1)}, u32[]{:S(2)}, u32[]{:S(2)}) %collective-permute-start.1) | collective-permute-done | bytes 589856 | tf_op jit(solution)/shard_map/ppermute | solution.py:13
  50.3 2.6 %collective-permute-done = bf16[256,1152]{1,0:T(8,128)(2,1)S(1)} collective-permute-done((bf16[256,1152]{1,0:T(8,128)(2,1)}, bf16[256,1152]{1,0:T(8,128)(2,1)S(1)}, u32[]{:S(2)}, u32[]{:S(2)}) %collective-permute-start) | collective-permute-done | bytes 589856 | tf_op jit(solution)/shard_map/ppermute | solution.py:13
  52.9 11.7 %all-gather.3.cloned.1.call-done = bf16[1,2,1152,1152]{3,2,1,0:T(8,128)(2,1)} async-done(((bf16[1,2,72,1152]{3,2,1,0:T(8,128)(2,1)}), bf16[1,2,1152,1152]{3,2,1,0:T(8,128)(2,1)}) %all-gather.3.cloned.1.call-update) | async-done | bytes 5308432 | tf_op jit(solution)/shard_map/all_gather | solution.py:50
  64.6 5.7 %multiply_reduce_fusion.3 = (f32[1024]{0:T(1024)S(1)}, f32[1024,1152]{1,0:T(8,128)S(1)}) fusion(bf16[1,2,1152,1152]{3,2,1,0:T(8,128)(2,1)} %all-gather.3.cloned.1.call-done, bf16[256,1152]{1,0:T(8,128)(2,1)S(1)} %collective-permute-done.2, bf16[256,1152]{1,0:T(8,128)(2,1)S(1)} %collective-permute-done.1, bf16[256,1152]{1,0:T(8,128)(2,1)S(1)} %collective-permute-done, ...), kind=kOutput, calls=%fused_computation.11 | convolution fusion | flops 2729704448 | bytes 9736192 | tf_op jit(solution)/shard_map/dot_general | solution.py:29
  70.3 4.7 %multiply_reduce_fusion.2 = (f32[1024]{0:T(1024)S(1)}, f32[1024,1152]{1,0:T(8,128)S(1)}) fusion(bf16[1,2,1152,1152]{3,2,1,0:T(8,128)(2,1)S(1)} %copy-done.1, bf16[256,1152]{1,0:T(8,128)(2,1)} %collective-permute-done.5, bf16[256,1152]{1,0:T(8,128)(2,1)S(1)} %collective-permute-done.4, bf16[256,1152]{1,0:T(8,128)(2,1)S(1)} %collective-permute-done.3, ...), kind=kOutput, calls=%fused_computation.10 | convolution fusion | flops 2729704448 | bytes 9736192 | tf_op jit(solution)/shard_map/dot_general | solution.py:29
  75.1 4.1 %multiply_convert_fusion = bf16[1024,1024]{1,0:T(8,128)(2,1)S(1)} fusion(f32[]{:T(128)} %bitcast.5, f32[]{:T(128)} %bitcast.1, pred[1024]{0:T(1024)(128)(4,1)S(1)} %iota_compare_fusion.1, f32[1024,1152]{1,0:T(8,128)S(1)} %get-tuple-element.12, f32[1024]{0:T(1024)S(1)} %add_sqrt_fusion.1, f32[1024,1152]{1,0:T(8,128)S(1)} %get-tuple-element.14, ...), kind=kOutput, calls=%fused_computation.12 | convolution fusion | flops 2433220608 | bytes 11543560 | tf_op jit(solution)/shard_map/dot_general | solution.py:29
  79.2 3.3 %multiply_reduce_fusion.1 = (f32[1024]{0:T(1024)S(1)}, f32[1024,1152]{1,0:T(8,128)S(1)}) fusion(f32[1024,1152]{1,0:T(8,128)S(1)} %get-tuple-element.12, f32[1024]{0:T(1024)S(1)} %add_sqrt_fusion.1, bf16[1024,1024]{1,0:T(8,128)(2,1)S(1)} %multiply_convert_fusion, f32[1024,1152]{1,0:T(8,128)S(1)} %get-tuple-element.14, f32[1024]{0:T(1024)S(1)} %add_sqrt_fusion, ...), kind=kOutput, calls=%fused_computation.9 | convolution fusion | flops 2422995968 | bytes 16265220 | tf_op jit(solution)/shard_map/dot_general | solution.py:29
  82.5 3.7 %multiply_reduce_fusion = (f32[1024]{0:T(1024)S(1)}, f32[1024,1152]{1,0:T(8,128)S(1)}) fusion(f32[1024,1152]{1,0:T(8,128)S(1)} %get-tuple-element.14, f32[1024]{0:T(1024)S(1)} %add_sqrt_fusion, bf16[1024,1024]{1,0:T(8,128)(2,1)S(1)} %multiply_convert_fusion, f32[1024,1152]{1,0:T(8,128)S(1)} %get-tuple-element.12, f32[1024]{0:T(1024)S(1)} %add_sqrt_fusion.1, ...), kind=kOutput, calls=%fused_computation.7 | convolution fusion | flops 2422995968 | bytes 16265220 | tf_op jit(solution)/shard_map/dot_general | solution.py:29
  86.2 3.5 %convolution_convert_fusion.1 = bf16[1152,1152]{1,0:T(8,128)(2,1)S(1)} fusion(f32[1024,1152]{1,0:T(8,128)S(1)} %get-tuple-element.18, f32[1024]{0:T(1024)S(1)} %get-tuple-element.17, f32[1024]{0:T(1024)S(1)} %add_sqrt_fusion.1, bf16[256,1152]{1,0:T(8,128)(2,1)S(1)} %collective-permute-done.2, bf16[256,1152]{1,0:T(8,128)(2,1)S(1)} %collective-permute-done.1, ...), kind=kOutput, calls=%fused_computation.1 | convolution fusion | flops 2734571520 | bytes 14458880 | tf_op jit(solution)/shard_map/dot_general | solution.py:29
  89.7 4.8 %broadcast_select_fusion = (bf16[1152,1152]{1,0:T(8,128)(2,1)S(1)}, bf16[1152,1152]{1,0:T(8,128)(2,1)S(1)}) fusion(bf16[1152,1152]{1,0:T(8,128)(2,1)S(1)} %convolution_convert_fusion.1, pred[]{:T(512)S(6)} %eq.8, f32[1024,1152]{1,0:T(8,128)S(1)} %get-tuple-element.16, f32[1024]{0:T(1024)S(1)} %get-tuple-element.15, f32[1024]{0:T(1024)S(1)} %add_sqrt_fusion, ...), kind=kOutput, calls=%fused_computation.19 | convolution fusion | flops 2735898624 | bytes 19767296 | tf_op jit(solution)/shard_map/dot_general | solution.py:29
  94.6 0.3 collective-permute-start.6
  94.9 4.7 %collective-permute-done.6 = bf16[1152,1152]{1,0:T(8,128)(2,1)S(1)} collective-permute-done((bf16[1152,1152]{1,0:T(8,128)(2,1)S(1)}, bf16[1152,1152]{1,0:T(8,128)(2,1)S(1)}, u32[]{:S(2)}, u32[]{:S(2)}) %collective-permute-start.6) | collective-permute-done | bytes 2654240 | tf_op jit(solution)/shard_map/ppermute | solution.py:21
  99.6 2.5 %add_convert_fusion = bf16[1152,1152]{1,0:T(8,128)(2,1)} fusion(bf16[1152,1152]{1,0:T(8,128)(2,1)S(1)} %collective-permute-done.6, bf16[1152,1152]{1,0:T(8,128)(2,1)S(1)} %convolution_convert_fusion.1, bf16[1152,1152]{1,0:T(8,128)(2,1)S(1)} %get-tuple-element.20, pred[]{:T(512)S(6)} %eq.8), kind=kLoop, calls=%fused_computation.3 | loop fusion | flops 6635520 | bytes 10616833 | tf_op jit(solution)/shard_map/convert_element_type | solution.py:73
  102.1 5.3 %all-to-all-start = ((bf16[8,144,1152]{2,1,0:T(8,128)(2,1)}), bf16[8,144,1152]{2,1,0:T(8,128)(2,1)S(1)}, u32[]{:S(2)}, u32[]{:S(2)}) async-start(bf16[8,144,1152]{2,1,0:T(8,128)(2,1)} %bitcast.45), calls=%async_computation | async-start | bytes 5308416 | tf_op jit(solution)/shard_map/all_to_all | solution.py:25
  107.4 0.1 collective-permute-start.7
  107.5 1.4 collective-permute-done.7
  109.0 29.7 %all-to-all-done = bf16[8,144,1152]{2,1,0:T(8,128)(2,1)S(1)} async-done(((bf16[8,144,1152]{2,1,0:T(8,128)(2,1)}), bf16[8,144,1152]{2,1,0:T(8,128)(2,1)S(1)}, u32[]{:S(2)}, u32[]{:S(2)}) %all-to-all-start) | async-done | bytes 2654240 | tf_op jit(solution)/shard_map/all_to_all | solution.py:25
  138.6 0.4 convert_reduce_fusion
  139.0 0.1 add_convert_fusion.1
  139.1 25.3 %all_to_all.15 = bf16[16,88,128]{2,1,0:T(8,128)(2,1)S(1)} all-to-all(bf16[16,88,128]{2,1,0:T(8,128)(2,1)S(1)} %bitcast.49), channel_id=1, replica_groups=mesh['z'=8,'xh'=2,'xl'=2,'y'=4,'c'=2] {'z','xh'}, dimensions={0} | all-to-all | bytes 720896 | tf_op jit(solution)/shard_map/all_to_all | solution.py:25
  164.6 25.0 %all_to_all.16 = f32[16,88,128]{2,1,0:T(8,128)S(1)} all-to-all(f32[16,88,128]{2,1,0:T(8,128)S(1)} %broadcast_in_dim.20), channel_id=1, replica_groups=mesh['z'=8,'xh'=2,'xl'=2,'y'=4,'c'=2] {'z','xh'}, dimensions={0} | all-to-all | bytes 1441792 | tf_op jit(solution)/shard_map/all_to_all | solution.py:25
  189.7 0.1 collective-permute-start.8
  189.8 1.6 collective-permute-done.8
  191.5 0.9 pad_maximum_fusion.2
  (25 shorter events, 0.4 us)
Async XLA Ops:
  6.5 58.1 %all-gather.3.cloned.1.call-start = ((), (), s32[]{:S(2)}) async-start(), calls=%async_computation.3 | async-start | bytes 5640192 | tf_op jit(solution)/shard_map/all_gather | solution.py:50
  7.3 15.4 %collective-permute-start.4 = (bf16[256,1152]{1,0:T(8,128)(2,1)}, bf16[256,1152]{1,0:T(8,128)(2,1)S(1)}, u32[]{:S(2)}, u32[]{:S(2)}) collective-permute-start(bf16[256,1152]{1,0:T(8,128)(2,1)} %bitcast.56), channel_id=1, source_target_pairs={{0,8},{8,0},{1,9},{9,1},{2,10},{10,2},{3,11},{11,3},{4,12},{12,4},... | collective-permute-start | bytes 1769480 | tf_op jit(solution)/shard_map/ppermute | solution.py:17
  8.8 18.4 %collective-permute-start.2 = (bf16[256,1152]{1,0:T(8,128)(2,1)}, bf16[256,1152]{1,0:T(8,128)(2,1)S(1)}, u32[]{:S(2)}, u32[]{:S(2)}) collective-permute-start(bf16[256,1152]{1,0:T(8,128)(2,1)} %bitcast.51), channel_id=1, source_target_pairs={{0,4},{2,6},{4,0},{6,2},{1,5},{3,7},{5,1},{7,3},{8,12},{10,14},{12... | collective-permute-start | bytes 1769480 | tf_op jit(solution)/shard_map/ppermute | solution.py:13
  11.1 39.2 %collective-permute-start.1 = (bf16[256,1152]{1,0:T(8,128)(2,1)}, bf16[256,1152]{1,0:T(8,128)(2,1)S(1)}, u32[]{:S(2)}, u32[]{:S(2)}) collective-permute-start(bf16[256,1152]{1,0:T(8,128)(2,1)} %bitcast.52), channel_id=1, source_target_pairs={{0,6},{2,0},{4,2},{6,4},{1,7},{3,1},{5,3},{7,5},{8,14},{10,8},{12,... | collective-permute-start | bytes 1769480 | tf_op jit(solution)/shard_map/ppermute | solution.py:13
  12.5 40.5 %collective-permute-start = (bf16[256,1152]{1,0:T(8,128)(2,1)}, bf16[256,1152]{1,0:T(8,128)(2,1)S(1)}, u32[]{:S(2)}, u32[]{:S(2)}) collective-permute-start(bf16[256,1152]{1,0:T(8,128)(2,1)} %bitcast.53), channel_id=1, source_target_pairs={{0,2},{2,4},{4,6},{6,0},{1,3},{3,5},{5,7},{7,1},{8,10},{10,12},{12... | collective-permute-start | bytes 1769480 | tf_op jit(solution)/shard_map/ppermute | solution.py:13
  13.2 57.1 %collective-permute-start.3 = (bf16[256,1152]{1,0:T(8,128)(2,1)}, bf16[256,1152]{1,0:T(8,128)(2,1)S(1)}, u32[]{:S(2)}, u32[]{:S(2)}) collective-permute-start(bf16[256,1152]{1,0:T(8,128)(2,1)} %bitcast.57), channel_id=1, source_target_pairs={{0,1},{1,0},{2,3},{3,2},{4,5},{5,4},{6,7},{7,6},{8,9},{9,8},{10,11... | collective-permute-start | bytes 1769480 | tf_op jit(solution)/shard_map/ppermute | solution.py:21
  15.2 55.1 %copy-start.3 = (bf16[1,256,1152]{2,1,0:T(8,128)(2,1)S(1)}, bf16[1,256,1152]{2,1,0:T(8,128)(2,1)}, u32[]{:S(2)}) copy-start(bf16[1,256,1152]{2,1,0:T(8,128)(2,1)} %param.6) | copy-start | bytes 1769476
  22.6 47.7 %collective-permute-start.5 = (bf16[256,1152]{1,0:T(8,128)(2,1)S(1)}, bf16[256,1152]{1,0:T(8,128)(2,1)}, u32[]{:S(2)}, u32[]{:S(2)}) collective-permute-start(bf16[256,1152]{1,0:T(8,128)(2,1)S(1)} %collective-permute-done.4), channel_id=1, source_target_pairs={{0,1},{1,0},{2,3},{3,2},{4,5},{5,4},{6,7},{7,6},{8,9},{9,8},{10,11... | collective-permute-start | bytes 1769480 | tf_op jit(solution)/shard_map/ppermute | solution.py:21
  64.6 5.7 %copy-start.1 = (bf16[1,2,1152,1152]{3,2,1,0:T(8,128)(2,1)S(1)}, bf16[1,2,1152,1152]{3,2,1,0:T(8,128)(2,1)}, u32[]{:S(2)}) copy-start(bf16[1,2,1152,1152]{3,2,1,0:T(8,128)(2,1)} %all-gather.3.cloned.1.call-done) | copy-start | bytes 15925252
  82.5 3.7 %copy-start.2 = (bf16[1,256,1152]{2,1,0:T(8,128)(2,1)S(1)}, bf16[1,256,1152]{2,1,0:T(8,128)(2,1)}, u32[]{:S(2)}) copy-start(bf16[1,256,1152]{2,1,0:T(8,128)(2,1)} %param.5) | copy-start | bytes 1769476
  94.6 5.0 %collective-permute-start.6 = (bf16[1152,1152]{1,0:T(8,128)(2,1)S(1)}, bf16[1152,1152]{1,0:T(8,128)(2,1)S(1)}, u32[]{:S(2)}, u32[]{:S(2)}) collective-permute-start(bf16[1152,1152]{1,0:T(8,128)(2,1)S(1)} %get-tuple-element.19), channel_id=1, source_target_pairs={{0,1},{1,0},{2,3},{3,2},{4,5},{5,4},{6,7},{7,6},{8,9},{9,8},{10,11... | collective-permute-start | bytes 7962632 | tf_op jit(solution)/shard_map/ppermute | solution.py:21
  102.1 5.3 %copy-start = (bf16[1,2,72,1152]{3,2,1,0:T(8,128)(2,1)S(1)}, bf16[1,2,72,1152]{3,2,1,0:T(8,128)(2,1)}, u32[]{:S(2)}) copy-start(bf16[1,2,72,1152]{3,2,1,0:T(8,128)(2,1)} %param.8) | copy-start | bytes 995332
  102.1 36.5 %all-to-all-start = ((bf16[8,144,1152]{2,1,0:T(8,128)(2,1)}), bf16[8,144,1152]{2,1,0:T(8,128)(2,1)S(1)}, u32[]{:S(2)}, u32[]{:S(2)}) async-start(bf16[8,144,1152]{2,1,0:T(8,128)(2,1)} %bitcast.45), calls=%async_computation | async-start | bytes 5308416 | tf_op jit(solution)/shard_map/all_to_all | solution.py:25
  107.4 1.5 collective-permute-start.7
  189.7 1.7 collective-permute-start.8
Sparse Core Ops, SparseCore 0:
  9.2 55.4 all-gather.2

commit v2 on v1

v2 whole, which is shorter than its diff:
```python
import jax
import jax.numpy as jnp
from jax import lax
from jax.sharding import Mesh, PartitionSpec as P

BF = jnp.bfloat16
F32 = jnp.float32
CHIPS = ("xl", "y")
GROUP = ("z", "xh")


def shift_y(x, by):
    return lax.ppermute(x, "y", [(i, (i + by) % 4) for i in range(4)])


def swap_x(x):
    return lax.ppermute(x, "xl", [(0, 1), (1, 0)])


def swap_core(x):
    return lax.ppermute(x, "c", [(0, 1), (1, 0)])


def exchange(x, axes):
    return lax.all_to_all(x, axes, split_axis=0, concat_axis=0, tiled=True)


def dot(a, b, dims):
    return lax.dot_general(a, b, (dims, ((), ())), preferred_element_type=F32)


def embed(x, w):
    u = dot(x, w, ((1,), (0,)))
    nrm = jnp.sqrt(jnp.sum(u * u, axis=1, keepdims=True) + 1e-06)
    return u / nrm, nrm


def back_norm(unit, nrm, dz):
    return ((dz - unit * jnp.sum(unit * dz, axis=1, keepdims=True)) / nrm).astype(BF)


def local(img_feat, txt_feat, group_weights, drift, logit_params):
    core = lax.axis_index("c")
    x_img, x_txt = img_feat[0], txt_feat[0]
    rows = x_img.shape[0]
    scale = jnp.exp(logit_params[0])
    bias = logit_params[1]

    weights = lax.all_gather(group_weights[0], ("xl", "y", "c"), axis=1, tiled=True)
    txt_x = swap_x(x_txt)
    below, above = shift_y(x_img, 1), shift_y(x_img, 3)
    half = rows // 2
    x_img = jnp.concatenate([x_img, below, above, shift_y(below[:half], 1), shift_y(above[half:], 3)], 0)
    x_txt = jnp.concatenate([x_txt, swap_core(x_txt), txt_x, swap_core(txt_x)], 0)

    def columns(x):
        parts = x.T.reshape(8, 2, -1, x.shape[0])
        pick = lambda k: lax.dynamic_index_in_dim(parts, k, 1, keepdims=False).reshape(-1, x.shape[0])
        return pick(core), pick(1 - core)

    keep_img, give_img = columns(x_img)
    keep_txt, give_txt = columns(x_txt)

    zf_txt, n_txt = embed(x_txt, weights[1])
    zf_img, n_img = embed(x_img, weights[0])
    z_img, z_txt = zf_img.astype(BF), zf_txt.astype(BF)
    score = scale * dot(z_img, z_txt, ((1,), (1,))) + bias
    i = lax.broadcasted_iota(jnp.int32, score.shape, 0)
    j = lax.broadcasted_iota(jnp.int32, score.shape, 1)
    label = jnp.where((i == j) & (i < rows), 1.0, -1.0).astype(F32)
    gb = (-label * jax.nn.sigmoid(-label * score)).astype(BF)
    nn = ((1,), (0,))
    du_txt = back_norm(zf_txt, n_txt, scale * dot(gb, z_img, ((0,), (0,))))
    got_txt = swap_core(dot(give_txt, du_txt, nn).astype(BF))
    du_img = back_norm(zf_img, n_img, scale * dot(gb, z_txt, nn))
    got_img = swap_core(dot(give_img, du_img, nn).astype(BF))
    g_txt = dot(keep_txt, du_txt, nn)
    g_img = dot(keep_img, du_img, nn)
    d, e = g_img.shape
    h = d // 8
    sums = [(g + got.astype(F32)).astype(BF).reshape(8, h, e) for g, got in ((g_img, got_img), (g_txt, got_txt))]
    parts = exchange(jnp.stack(sums, 1), CHIPS)
    block = jnp.sum(parts.astype(F32), axis=0) + drift[0].astype(F32)
    tiles = block.reshape(2 * h // 8, 8, e // 128, 128).transpose(0, 2, 1, 3).reshape(-1, 8, 128)
    n = tiles.shape[0]
    each = -(-n // 16)
    tiles = jnp.pad(tiles, ((0, 16 * each - n), (0, 0), (0, 0))).reshape(16, each * 8, 128)
    total = jnp.sum(exchange(tiles.astype(BF), GROUP).astype(F32), axis=0) * (1.0 / 16)
    out = exchange(jnp.broadcast_to(total.astype(BF)[None], (16, each * 8, 128)), GROUP).astype(F32)
    out = out.reshape(16 * each, 8, 128)[:n].reshape(2 * h // 8, e // 128, 8, 128).transpose(0, 2, 1, 3)
    return out.reshape(2, h, e)


def solution(mesh):
    fine = Mesh(mesh.devices.reshape(8, 2, 2, 4, 2), ("z", "xh", "xl", "y", "c"))
    dp = ("xl", "y", "c")
    return jax.shard_map(
        local,
        mesh=fine,
        in_specs=(
            P(GROUP, dp, None),
            P(GROUP, dp, None),
            P(GROUP, None, dp, None),
            P(GROUP, None, dp, None),
            P(),
        ),
        out_specs=P(None, dp, None),
        check_vma=False,
    )
```

time: 203 us -> 183 us (0.901); the launches traced: 199 us -> 182 us
  waiting for transfers between devices: 87.5 us -> 37.7 us
  blocking collectives: 50.3 us -> 78.8 us
  local copies, waits for them, and re-layouts: 1.47 us -> 11.1 us
  starting transfers between devices: 11.7 us -> 6.81 us
    all_to_all x1 -> x0, waiting for transfers between devices: 29.7 us -> none  [exchange(): return lax.all_to_all(x, axes, split_axis=0, concat_axis=0, tiled=True)]
    all_to_all x2 -> x3, blocking collectives: 50.3 us -> 78.8 us  [exchange(): return lax.all_to_all(x, axes, split_axis=0, concat_axis=0, tiled=True)]
    ppermute x1, waiting for transfers between devices: 7.4 us -> 0.01 us  [swap_x(): return lax.ppermute(x, 'xl', [(0, 1), (1, 0)])]
    ppermute x5 -> x4, waiting for transfers between devices: 7.74 us -> 1.06 us  [swap_core(): return lax.ppermute(x, 'c', [(0, 1), (1, 0)])]
    unnamed x8 -> x20, local copies, waits for them, and re-layouts: 0.02 us -> 5.93 us
    all_to_all x1 -> x0, starting transfers between devices: 5.28 us -> none  [exchange(): return lax.all_to_all(x, axes, split_axis=0, concat_axis=0, tiled=True)]
    all_gather x1, waiting for transfers between devices: 11.7 us -> 8.18 us  [local(): lax.all_gather(group_weights[0], ('xl', 'y', 'c'), axis=1, tiled=True)]
    ppermute x3 -> x4, waiting for transfers between devices: 30.3 us -> 27.7 us  [shift_y(): return lax.ppermute(x, 'y', [(i, (i + by) % 4) for i in range(4)])]
  transfers between devices with their start and end apart: 11 -> 10, of which waited for: 9 -> 5; matrix products, arithmetic and copies ran while one was open for 4% -> 9% of each run, Pallas kernels for 0% -> 0%
where the time goes in v2:
time: 183 us; the launch traced here: 182 us
  blocking collectives  78.8 us (43%)
  waiting for transfers between devices  37.7 us (21%)
  matrix products  28 us (15%)
  between operations  14.3 us (8%)
  local copies, waits for them, and re-layouts  11.1 us (6%)
  starting transfers between devices  6.81 us (4%)
  other arithmetic  5.52 us (3%)
    all_to_all x3, blocking collectives, exchange(): return lax.all_to_all(x, axes, split_axis=0, concat_axis=0, tiled=True)  78.8 us
    dot_general x9, matrix products, dot(): return lax.dot_general(a, b, (dims, ((), ())), preferred_element_type=F32)  28 us
    ppermute x4, waiting for transfers between devices, shift_y(): return lax.ppermute(x, 'y', [(i, (i + by) % 4) for i in range(4)])  27.7 us
    all_gather x1, waiting for transfers between devices, local(): lax.all_gather(group_weights[0], ('xl', 'y', 'c'), axis=1, tiled=True)  8.18 us
    unnamed x20, local copies, waits for them, and re-layouts  5.93 us
    ppermute x4, starting transfers between devices, shift_y(): return lax.ppermute(x, 'y', [(i, (i + by) % 4) for i in range(4)])  4.28 us
  transfers between devices with their start and end apart: 10, of which 5 were waited for; matrix products, arithmetic and copies ran while one was open for 9% of the time, Pallas kernels for 0%

profile of v2, /device:TPU:8, one launch (start us, length us, event | category | flops | bytes accessed | tf_op | source)
XLA Modules:
  0.0 182.3 jit_solution(11434702603955659412)
XLA Ops:
  6.5 0.7 all-gather.3.cloned.1.call-update
  7.3 1.3 copy.9
  8.6 1.6 collective-permute-start.5
  10.1 1.3 copy.8
  11.4 1.7 collective-permute-start
  15.0 15.2 %collective-permute-done = bf16[256,1152]{0,1:T(8,128)(2,1)} collective-permute-done((bf16[256,1152]{0,1:T(8,128)(2,1)S(1)}, bf16[256,1152]{0,1:T(8,128)(2,1)}, u32[]{:S(2)}, u32[]{:S(2)}) %collective-permute-start) | collective-permute-done | bytes 589856 | tf_op jit(solution)/shard_map/ppermute | solution.py:13
  30.2 1.0 slice.31
  31.2 1.6 collective-permute-start.2
  32.9 1.0 slice.32
  34.4 1.2 constant_dynamic-update-slice_fusion.3
  35.6 1.1 constant_dynamic-update-slice_fusion.2
  36.7 9.7 %collective-permute-done.2 = bf16[128,1152]{0,1:T(8,128)(2,1)S(1)} collective-permute-done((bf16[128,1152]{0,1:T(8,128)(2,1)S(1)}, bf16[128,1152]{0,1:T(8,128)(2,1)S(1)}, u32[]{:S(2)}, u32[]{:S(2)}) %collective-permute-start.2) | collective-permute-done | bytes 294944 | tf_op jit(solution)/shard_map/ppermute | solution.py:13
  46.6 2.8 %collective-permute-done.3 = bf16[128,1152]{0,1:T(8,128)(2,1)S(1)} collective-permute-done((bf16[128,1152]{0,1:T(8,128)(2,1)S(1)}, bf16[128,1152]{0,1:T(8,128)(2,1)S(1)}, u32[]{:S(2)}, u32[]{:S(2)}) %collective-permute-start.3) | collective-permute-done | bytes 294944 | tf_op jit(solution)/shard_map/ppermute | solution.py:13
  49.4 1.6 pad_maximum_fusion.1
  51.0 2.4 %constant_dynamic-slice_fusion = (bf16[8,1,72,1024]{3,2,1,0:T(8,128)(2,1)}, bf16[8,1,72,1024]{3,2,1,0:T(8,128)(2,1)}, bf16[8,1,72,1024]{3,2,1,0:T(8,128)(2,1)}, bf16[8,1,72,1024]{3,2,1,0:T(8,128)(2,1)}) fusion(bf16[8,2,72,1024]{3,2,1,0:T(8,128)(2,1)S(1)} %bitcast.55, s32[]{:T(128)S(6)} %select_n.17, s32[]{:T(128)S(6)} %select_n.15, ...), kind=kLoop, calls=%fused_computation.41 | loop fusion | bytes 9437192 | tf_op jit(solution)/shard_map/jit(dynamic_index_in_dim)/dynamic_slice | solution.py:58
  53.4 8.2 %all-gather.3.cloned.1.call-done = bf16[1,2,1152,1152]{3,2,1,0:T(8,128)(2,1)} async-done(((bf16[1,2,72,1152]{3,2,1,0:T(8,128)(2,1)}), bf16[1,2,1152,1152]{3,2,1,0:T(8,128)(2,1)}) %all-gather.3.cloned.1.call-update) | async-done | bytes 5308432 | tf_op jit(solution)/shard_map/all_gather | solution.py:49
  61.6 6.0 %multiply_reduce_fusion.2 = (f32[1024]{0:T(1024)S(1)}, f32[1024,1152]{1,0:T(8,128)S(1)}) fusion(bf16[1,2,1152,1152]{3,2,1,0:T(8,128)(2,1)} %all-gather.3.cloned.1.call-done, bf16[256,1152]{0,1:T(8,128)(2,1)S(1)} %collective-permute-done.6, bf16[256,1152]{0,1:T(8,128)(2,1)} %collective-permute-done.5, bf16[256,1152]{0,1:T(8,128)(2,1)} %collective-permute-done.4, ...), kind=kOutput, calls=%fused_computation.7 | convolution fusion | flops 2729704448 | bytes 9736192 | tf_op jit(solution)/shard_map/dot_general | solution.py:29
  67.6 3.8 %multiply_reduce_fusion.3 = (f32[1024]{0:T(1024)S(1)}, f32[1024,1152]{1,0:T(8,128)S(1)}) fusion(bf16[1024,1152]{0,1:T(8,128)(2,1)S(1)} %constant_dynamic-update-slice_fusion, bf16[1,2,1152,1152]{3,2,1,0:T(8,128)(2,1)S(1)} %copy-done.6), kind=kOutput, calls=%fused_computation.8 | convolution fusion | flops 2720267264 | bytes 9736192 | tf_op jit(solution)/shard_map/dot_general | solution.py:29
  71.5 4.1 %multiply_convert_fusion = bf16[1024,1024]{1,0:T(8,128)(2,1)S(1)} fusion(f32[]{:T(128)} %bitcast.8, f32[]{:T(128)} %bitcast.4, pred[1024]{0:T(1024)(128)(4,1)S(1)} %iota_compare_fusion.1, f32[1024,1152]{1,0:T(8,128)S(1)} %get-tuple-element.12, f32[1024]{0:T(1024)S(1)} %add_sqrt_fusion.1, f32[1024,1152]{1,0:T(8,128)S(1)} %get-tuple-element.14, ...), kind=kOutput, calls=%fused_computation.9 | convolution fusion | flops 2433220608 | bytes 11543560 | tf_op jit(solution)/shard_map/dot_general | solution.py:29
  75.6 3.6 %multiply_reduce_fusion.1 = (f32[1024]{0:T(1024)S(1)}, f32[1024,1152]{1,0:T(8,128)S(1)}) fusion(f32[1024,1152]{1,0:T(8,128)S(1)} %get-tuple-element.12, f32[1024]{0:T(1024)S(1)} %add_sqrt_fusion.1, bf16[1024,1024]{1,0:T(8,128)(2,1)S(1)} %multiply_convert_fusion, f32[1024,1152]{1,0:T(8,128)S(1)} %get-tuple-element.14, f32[1024]{0:T(1024)S(1)} %add_sqrt_fusion, ...), kind=kOutput, calls=%fused_computation.6 | convolution fusion | flops 2422995968 | bytes 16265220 | tf_op jit(solution)/shard_map/dot_general | solution.py:29
  79.2 3.6 %multiply_reduce_fusion = (f32[1024]{0:T(1024)S(1)}, f32[1024,1152]{1,0:T(8,128)S(1)}) fusion(f32[1024,1152]{1,0:T(8,128)S(1)} %get-tuple-element.14, f32[1024]{0:T(1024)S(1)} %add_sqrt_fusion, bf16[1024,1024]{1,0:T(8,128)(2,1)S(1)} %multiply_convert_fusion, f32[1024,1152]{1,0:T(8,128)S(1)} %get-tuple-element.12, f32[1024]{0:T(1024)S(1)} %add_sqrt_fusion.1, ...), kind=kOutput, calls=%fused_computation.4 | convolution fusion | flops 2422995968 | bytes 16265220 | tf_op jit(solution)/shard_map/dot_general | solution.py:29
  82.8 1.1 divide_convert_fusion.1
  84.1 1.7 convolution_convert_fusion.1
  86.1 1.1 divide_convert_fusion
  87.4 1.7 convolution_convert_fusion
  89.7 1.7 fusion.1
  91.5 1.1 collective-permute-done.8
  92.5 1.7 add_convert_fusion
  94.5 36.5 %all_to_all.15 = bf16[8,2,72,1152]{3,2,1,0:T(8,128)(2,1)S(1)} all-to-all(bf16[8,2,72,1152]{3,2,1,0:T(8,128)(2,1)S(1)} %pad_maximum_fusion), channel_id=1, replica_groups=mesh['z'=8,'xh'=2,'xl'=2,'y'=4,'c'=2] {'xl','y'}, dimensions={0} | all-to-all | bytes 5308416 | tf_op jit(solution)/shard_map/all_to_all | solution.py:25
  132.1 25.4 %all_to_all.16 = bf16[16,88,128]{2,1,0:T(8,128)(2,1)S(1)} all-to-all(bf16[16,88,128]{2,1,0:T(8,128)(2,1)S(1)} %bitcast.64), channel_id=1, replica_groups=mesh['z'=8,'xh'=2,'xl'=2,'y'=4,'c'=2] {'z','xh'}, dimensions={0} | all-to-all | bytes 720896 | tf_op jit(solution)/shard_map/all_to_all | solution.py:25
  157.6 16.9 %all_to_all.17 = bf16[16,88,128]{2,1,0:T(8,128)(2,1)S(1)} all-to-all(bf16[16,88,128]{2,1,0:T(8,128)(2,1)S(1)} %broadcast_in_dim.20), channel_id=1, replica_groups=mesh['z'=8,'xh'=2,'xl'=2,'y'=4,'c'=2] {'z','xh'}, dimensions={0} | all-to-all | bytes 720896 | tf_op jit(solution)/shard_map/all_to_all | solution.py:25
  174.6 0.9 convert.14
  (41 shorter events, 4.6 us)
Async XLA Ops:
  6.5 7.0 %copy-start.5 = (f32[2]{0:T(128)S(1)}, f32[2]{0:T(128)}, u32[]{:S(2)}) copy-start(f32[2]{0:T(128)} %param.9) | copy-start | bytes 28
  6.5 55.0 %all-gather.3.cloned.1.call-start = ((), (), s32[]{:S(2)}) async-start(), calls=%async_computation.3 | async-start | bytes 5640192 | tf_op jit(solution)/shard_map/all_gather | solution.py:49
  8.6 25.8 %collective-permute-start.5 = (bf16[256,1152]{0,1:T(8,128)(2,1)S(1)}, bf16[256,1152]{0,1:T(8,128)(2,1)}, u32[]{:S(2)}, u32[]{:S(2)}) collective-permute-start(bf16[256,1152]{0,1:T(8,128)(2,1)S(1)} %bitcast.58), channel_id=1, source_target_pairs={{0,8},{8,0},{1,9},{9,1},{2,10},{10,2},{3,11},{11,3},{4,12},{12,4},... | collective-permute-start | bytes 1769480 | tf_op jit(solution)/shard_map/ppermute | solution.py:17
  10.1 39.3 %collective-permute-start.4 = (bf16[256,1152]{0,1:T(8,128)(2,1)S(1)}, bf16[256,1152]{0,1:T(8,128)(2,1)}, u32[]{:S(2)}, u32[]{:S(2)}) collective-permute-start(bf16[256,1152]{0,1:T(8,128)(2,1)S(1)} %bitcast.59), channel_id=1, source_target_pairs={{0,1},{1,0},{2,3},{3,2},{4,5},{5,4},{6,7},{7,6},{8,9},{9,8},{10,11... | collective-permute-start | bytes 1769480 | tf_op jit(solution)/shard_map/ppermute | solution.py:21
  11.4 18.8 %collective-permute-start = (bf16[256,1152]{0,1:T(8,128)(2,1)S(1)}, bf16[256,1152]{0,1:T(8,128)(2,1)}, u32[]{:S(2)}, u32[]{:S(2)}) collective-permute-start(bf16[256,1152]{0,1:T(8,128)(2,1)S(1)} %bitcast.62), channel_id=1, source_target_pairs={{0,2},{2,4},{4,6},{6,0},{1,3},{3,5},{5,7},{7,1},{8,10},{10,12},{12... | collective-permute-start | bytes 1769480 | tf_op jit(solution)/shard_map/ppermute | solution.py:13
  13.1 19.8 %collective-permute-start.1 = (bf16[256,1152]{0,1:T(8,128)(2,1)S(1)}, bf16[256,1152]{0,1:T(8,128)(2,1)}, u32[]{:S(2)}, u32[]{:S(2)}) collective-permute-start(bf16[256,1152]{0,1:T(8,128)(2,1)S(1)} %bitcast.63), channel_id=1, source_target_pairs={{0,6},{2,0},{4,2},{6,4},{1,7},{3,1},{5,3},{7,5},{8,14},{10,8},{12,... | collective-permute-start | bytes 1769480 | tf_op jit(solution)/shard_map/ppermute | solution.py:13
  31.2 15.2 %collective-permute-start.2 = (bf16[128,1152]{0,1:T(8,128)(2,1)S(1)}, bf16[128,1152]{0,1:T(8,128)(2,1)S(1)}, u32[]{:S(2)}, u32[]{:S(2)}) collective-permute-start(bf16[128,1152]{0,1:T(8,128)(2,1)S(1)} %slice.31), channel_id=1, source_target_pairs={{0,2},{2,4},{4,6},{6,0},{1,3},{3,5},{5,7},{7,1},{8,10},{10,12},{12... | collective-permute-start | bytes 884744 | tf_op jit(solution)/shard_map/ppermute | solution.py:13
  33.8 15.5 %collective-permute-start.3 = (bf16[128,1152]{0,1:T(8,128)(2,1)S(1)}, bf16[128,1152]{0,1:T(8,128)(2,1)S(1)}, u32[]{:S(2)}, u32[]{:S(2)}) collective-permute-start(bf16[128,1152]{0,1:T(8,128)(2,1)S(1)} %slice.32), channel_id=1, source_target_pairs={{0,6},{2,0},{4,2},{6,4},{1,7},{3,1},{5,3},{7,5},{8,14},{10,8},{12,... | collective-permute-start | bytes 884744 | tf_op jit(solution)/shard_map/ppermute | solution.py:13
  34.4 15.1 %collective-permute-start.6 = (bf16[256,1152]{0,1:T(8,128)(2,1)}, bf16[256,1152]{0,1:T(8,128)(2,1)S(1)}, u32[]{:S(2)}, u32[]{:S(2)}) collective-permute-start(bf16[256,1152]{0,1:T(8,128)(2,1)} %collective-permute-done.5), channel_id=1, source_target_pairs={{0,1},{1,0},{2,3},{3,2},{4,5},{5,4},{6,7},{7,6},{8,9},{9,8},{10,11... | collective-permute-start | bytes 1769480 | tf_op jit(solution)/shard_map/ppermute | solution.py:21
  61.6 6.0 %copy-start.6 = (bf16[1,2,1152,1152]{3,2,1,0:T(8,128)(2,1)S(1)}, bf16[1,2,1152,1152]{3,2,1,0:T(8,128)(2,1)}, u32[]{:S(2)}) copy-start(bf16[1,2,1152,1152]{3,2,1,0:T(8,128)(2,1)} %all-gather.3.cloned.1.call-done) | copy-start | bytes 15925252
  82.8 1.3 copy-start.3
  85.8 3.9 %collective-permute-start.7 = (bf16[576,1152]{1,0:T(8,128)(2,1)S(1)}, bf16[576,1152]{1,0:T(8,128)(2,1)S(1)}, u32[]{:S(2)}, u32[]{:S(2)}) collective-permute-start(bf16[576,1152]{1,0:T(8,128)(2,1)S(1)} %convolution_convert_fusion.1), channel_id=1, source_target_pairs={{0,1},{1,0},{2,3},{3,2},{4,5},{5,4},{6,7},{7,6},{8,9},{9,8},{10,11... | collective-permute-start | bytes 3981320 | tf_op jit(solution)/shard_map/ppermute | solution.py:21
  86.1 1.3 copy-start.2
  87.4 2.3 %copy-start.1 = (bf16[8,1,72,1024]{3,2,1,0:T(8,128)(2,1)S(1)}, bf16[8,1,72,1024]{3,2,1,0:T(8,128)(2,1)}, u32[]{:S(2)}) copy-start(bf16[8,1,72,1024]{3,2,1,0:T(8,128)(2,1)} %get-tuple-element.19) | copy-start | bytes 3538948
  89.1 3.4 %collective-permute-start.8 = (bf16[576,1152]{1,0:T(8,128)(2,1)S(1)}, bf16[576,1152]{1,0:T(8,128)(2,1)S(1)}, u32[]{:S(2)}, u32[]{:S(2)}) collective-permute-start(bf16[576,1152]{1,0:T(8,128)(2,1)S(1)} %convolution_convert_fusion), channel_id=1, source_target_pairs={{0,1},{1,0},{2,3},{3,2},{4,5},{5,4},{6,7},{7,6},{8,9},{9,8},{10,11... | collective-permute-start | bytes 3981320 | tf_op jit(solution)/shard_map/ppermute | solution.py:21
  89.7 2.8 %copy-start = (bf16[8,1,72,1024]{3,2,1,0:T(8,128)(2,1)S(1)}, bf16[8,1,72,1024]{3,2,1,0:T(8,128)(2,1)}, u32[]{:S(2)}) copy-start(bf16[8,1,72,1024]{3,2,1,0:T(8,128)(2,1)} %get-tuple-element.8) | copy-start | bytes 3538948
  131.0 1.0 copy-start.4
Sparse Core Ops, SparseCore 0:
  9.2 52.3 all-gather.2

commit v3 on v2

--- a/solution.py
+++ b/solution.py
@@ -51,36 +51,51 @@
     below, above = shift_y(x_img, 1), shift_y(x_img, 3)
     half = rows // 2
     x_img = jnp.concatenate([x_img, below, above, shift_y(below[:half], 1), shift_y(above[half:], 3)], 0)
-    x_txt = jnp.concatenate([x_txt, swap_core(x_txt), txt_x, swap_core(txt_x)], 0)
+    x_half = jnp.concatenate([x_txt, txt_x], 0)
+    x_txt = jnp.concatenate([x_half, swap_core(x_half)], 0)
+
+    xl, y = lax.axis_index("xl"), lax.axis_index("y")
+    at = lambda v, k, axis: lax.dynamic_index_in_dim(v, k, axis, keepdims=False)
 
     def columns(x):
-        parts = x.T.reshape(8, 2, -1, x.shape[0])
-        pick = lambda k: lax.dynamic_index_in_dim(parts, k, 1, keepdims=False).reshape(-1, x.shape[0])
+        parts = x.T.reshape(2, 4, 2, -1, x.shape[0])
+        parts = jnp.concatenate([parts, parts], 1)
+        parts = lax.dynamic_slice_in_dim(parts, y, 4, 1)
+        parts = jnp.stack([at(parts, xl, 0), at(parts, 1 - xl, 0)])
+        pick = lambda k: at(parts, k, 2).reshape(-1, x.shape[0])
         return pick(core), pick(1 - core)
 
     keep_img, give_img = columns(x_img)
-    keep_txt, give_txt = columns(x_txt)
+    keep_txt, _ = columns(x_txt)
 
-    zf_txt, n_txt = embed(x_txt, weights[1])
+    zf_half, n_half = embed(x_half, weights[1])
+    z_half = zf_half.astype(BF)
+    z_txt = jnp.concatenate([z_half, swap_core(z_half)], 0)
+    n_txt = jnp.concatenate([n_half, swap_core(n_half)], 0)
     zf_img, n_img = embed(x_img, weights[0])
-    z_img, z_txt = zf_img.astype(BF), zf_txt.astype(BF)
+    z_img = zf_img.astype(BF)
     score = scale * dot(z_img, z_txt, ((1,), (1,))) + bias
     i = lax.broadcasted_iota(jnp.int32, score.shape, 0)
     j = lax.broadcasted_iota(jnp.int32, score.shape, 1)
     label = jnp.where((i == j) & (i < rows), 1.0, -1.0).astype(F32)
     gb = (-label * jax.nn.sigmoid(-label * score)).astype(BF)
     nn = ((1,), (0,))
-    du_txt = back_norm(zf_txt, n_txt, scale * dot(gb, z_img, ((0,), (0,))))
-    got_txt = swap_core(dot(give_txt, du_txt, nn).astype(BF))
+    du_txt = back_norm(z_txt.astype(F32), n_txt, scale * dot(gb, z_img, ((0,), (0,))))
+    got_txt = swap_core(jnp.concatenate([du_txt[2 * rows :], du_txt[: 2 * rows]], 0))
     du_img = back_norm(zf_img, n_img, scale * dot(gb, z_txt, nn))
     got_img = swap_core(dot(give_img, du_img, nn).astype(BF))
-    g_txt = dot(keep_txt, du_txt, nn)
+    g_txt = dot(keep_txt, (du_txt.astype(F32) + got_txt.astype(F32)).astype(BF), nn).astype(BF)
+    g_txt, got_img = lax.optimization_barrier((g_txt, got_img))
     g_img = dot(keep_img, du_img, nn)
     d, e = g_img.shape
     h = d // 8
-    sums = [(g + got.astype(F32)).astype(BF).reshape(8, h, e) for g, got in ((g_img, got_img), (g_txt, got_txt))]
-    parts = exchange(jnp.stack(sums, 1), CHIPS)
-    block = jnp.sum(parts.astype(F32), axis=0) + drift[0].astype(F32)
+    g_txt = g_txt.reshape(2, 4, h, e)
+    g_img = (g_img + got_img.astype(F32)).astype(BF).reshape(2, 4, h, e)
+    g_txt = (g_txt[0].astype(F32) + swap_x(g_txt[1]).astype(F32)).astype(BF)
+    g_img = sum([g_img[:, 0].astype(F32)] + [shift_y(g_img[:, k], k).astype(F32) for k in (1, 2, 3)]).astype(BF)
+    g_img = g_img[0].astype(F32) + swap_x(g_img[1]).astype(F32)
+    g_txt = sum([g_txt[0].astype(F32)] + [shift_y(g_txt[k], k).astype(F32) for k in (1, 2, 3)])
+    block = jnp.stack([g_img, g_txt]) + drift[0].astype(F32)
     tiles = block.reshape(2 * h // 8, 8, e // 128, 128).transpose(0, 2, 1, 3).reshape(-1, 8, 128)
     n = tiles.shape[0]
     each = -(-n // 16)

time: 183 us -> 174 us (0.951); the launches traced: 182 us -> 171 us
  blocking collectives: 78.8 us -> 39.5 us
  waiting for transfers between devices: 37.7 us -> 52.8 us
  starting transfers between devices: 6.81 us -> 15.5 us
  other arithmetic: 5.52 us -> 13.4 us
  matrix products: 28 us -> 23.4 us
    all_to_all x3 -> x2, blocking collectives: 78.8 us -> 39.5 us  [exchange(): return lax.all_to_all(x, axes, split_axis=0, concat_axis=0, tiled=True)]
    ppermute x4 -> x10, waiting for transfers between devices: 27.7 us -> 38.5 us  [shift_y(): return lax.ppermute(x, 'y', [(i, (i + by) % 4) for i in range(4)])]
    ppermute x1 -> x3, waiting for transfers between devices: 0.01 us -> 8.74 us  [swap_x(): return lax.ppermute(x, 'xl', [(0, 1), (1, 0)])]
    concatenate x1 -> x5, other arithmetic: 1.55 us -> 7.84 us  [the longest x1 4.06 us: columns(): parts = jnp.concatenate([parts, parts], 1)]
    ppermute x4 -> x10, starting transfers between devices: 4.28 us -> 10.3 us  [shift_y(): return lax.ppermute(x, 'y', [(i, (i + by) % 4) for i in range(4)])]
    dot_general x9 -> x8, matrix products: 28 us -> 23.4 us  [dot(): return lax.dot_general(a, b, (dims, ((), ())), preferred_element_type=F32)]
    all_gather x1, waiting for transfers between devices: 8.18 us -> 4.91 us  [local(): lax.all_gather(group_weights[0], ('xl', 'y', 'c'), axis=1, tiled=True)]
    unnamed x20, local copies, waits for them, and re-layouts: 5.93 us -> 9.04 us
  transfers between devices with their start and end apart: 10 -> 19, of which waited for: 5 -> 12; matrix products, arithmetic and copies ran while one was open for 9% -> 18% of each run, Pallas kernels for 0% -> 0%
where the time goes in v3:
time: 174 us; the launch traced here: 171 us
  waiting for transfers between devices  52.8 us (30%)
  blocking collectives  39.5 us (23%)
  matrix products  23.4 us (13%)
  starting transfers between devices  15.5 us (9%)
  between operations  14.4 us (8%)
  other arithmetic  13.4 us (8%)
  local copies, waits for them, and re-layouts  12.2 us (7%)
    all_to_all x2, blocking collectives, exchange(): return lax.all_to_all(x, axes, split_axis=0, concat_axis=0, tiled=True)  39.5 us
    ppermute x10, waiting for transfers between devices, shift_y(): return lax.ppermute(x, 'y', [(i, (i + by) % 4) for i in range(4)])  38.5 us
    dot_general x8, matrix products, dot(): return lax.dot_general(a, b, (dims, ((), ())), preferred_element_type=F32)  23.4 us
    ppermute x10, starting transfers between devices, shift_y(): return lax.ppermute(x, 'y', [(i, (i + by) % 4) for i in range(4)])  10.3 us
    unnamed x20, local copies, waits for them, and re-layouts  9.04 us
    ppermute x3, waiting for transfers between devices, swap_x(): return lax.ppermute(x, 'xl', [(0, 1), (1, 0)])  8.74 us
    all_gather x1, waiting for transfers between devices, local(): lax.all_gather(group_weights[0], ('xl', 'y', 'c'), axis=1, tiled=True)  4.91 us
    concatenate x1, other arithmetic, columns(): parts = jnp.concatenate([parts, parts], 1)  4.06 us
  transfers between devices with their start and end apart: 19, of which 12 were waited for; matrix products, arithmetic and copies ran while one was open for 18% of the time, Pallas kernels for 0%

profile of v3, /device:TPU:8, one launch (start us, length us, event | category | flops | bytes accessed | tf_op | source)
XLA Modules:
  0.0 171.4 jit_solution(13390994311852939581)
XLA Ops:
  7.3 1.3 copy.10
  8.6 1.6 collective-permute-start.4
  10.2 2.1 %copy.9 = bf16[1,256,1152]{1,2,0:T(8,128)(2,1)} copy(bf16[1,256,1152]{2,1,0:T(8,128)(2,1)} %param.5) | data formatting | bytes 1179648 | tf_op args[0]
  13.0 1.3 collective-permute-start
  14.3 1.2 constant_dynamic-update-slice_fusion.4
  15.5 8.2 %collective-permute-done.4 = bf16[256,1152]{0,1:T(8,128)(2,1)S(1)} collective-permute-done((bf16[256,1152]{0,1:T(8,128)(2,1)S(1)}, bf16[256,1152]{0,1:T(8,128)(2,1)S(1)}, u32[]{:S(2)}, u32[]{:S(2)}) %collective-permute-start.4) | collective-permute-done | bytes 589856 | tf_op jit(solution)/shard_map/ppermute | solution.py:17
  23.7 1.2 pad_maximum_fusion.3
  26.2 4.1 %collective-permute-done.1 = bf16[256,1152]{0,1:T(8,128)(2,1)} collective-permute-done((bf16[256,1152]{0,1:T(8,128)(2,1)}, bf16[256,1152]{0,1:T(8,128)(2,1)}, u32[]{:S(2)}, u32[]{:S(2)}) %collective-permute-start.1) | collective-permute-done | bytes 589856 | tf_op jit(solution)/shard_map/ppermute | solution.py:13
  31.7 2.7 %collective-permute-done = bf16[256,1152]{0,1:T(8,128)(2,1)} collective-permute-done((bf16[256,1152]{0,1:T(8,128)(2,1)}, bf16[256,1152]{0,1:T(8,128)(2,1)}, u32[]{:S(2)}, u32[]{:S(2)}) %collective-permute-start) | collective-permute-done | bytes 589856 | tf_op jit(solution)/shard_map/ppermute | solution.py:13
  37.8 12.1 %collective-permute-done.2 = bf16[128,1152]{0,1:T(8,128)(2,1)S(1)} collective-permute-done((bf16[128,1152]{0,1:T(8,128)(2,1)S(1)}, bf16[128,1152]{0,1:T(8,128)(2,1)S(1)}, u32[]{:S(2)}, u32[]{:S(2)}) %collective-permute-start.2) | collective-permute-done | bytes 294944 | tf_op jit(solution)/shard_map/ppermute | solution.py:13
  50.1 2.4 %pad_maximum_fusion.1 = bf16[1024,1152]{0,1:T(8,128)(2,1)S(1)} fusion(bf16[512,1152]{0,1:T(8,128)(2,1)} %collective-permute-done.6, bf16[256,1152]{0,1:T(8,128)(2,1)S(1)} %collective-permute-done.4, bf16[256,1152]{0,1:T(8,128)(2,1)S(1)} %bitcast.93), kind=kLoop, calls=%fused_computation.35 | loop fusion | flops 7077888 | bytes 4718592 | tf_op jit(solution)/shard_map/concatenate | solution.py:55
  52.6 4.1 %fusion.11 = (bf16[1,4,2,72,1024]{4,3,2,1,0:T(8,128)(2,1)}, bf16[1,4,2,72,1024]{4,3,2,1,0:T(8,128)(2,1)}, bf16[1,4,2,72,1024]{4,3,2,1,0:T(8,128)(2,1)S(1)}, bf16[1,4,2,72,1024]{4,3,2,1,0:T(8,128)(2,1)S(1)}) fusion(s32[]{:T(128)S(6)} %select_n.38, s32[]{:T(128)S(6)} %select_n.36, bf16[2,4,2,72,1024]{4,3,2,1,0:T(8,128)(2,1)S(1)} %bitcast.90, s32[]{:T(128)S(6)} %select_n.34, ...), kind=kLoop, calls=%fused_computation.47 | loop fusion | flops 2359296 | bytes 9437196 | tf_op jit(solution)/shard_map/concatenate | solution.py:62
  56.6 4.9 %all-gather.3.cloned.1.call-done = bf16[1,2,1152,1152]{3,2,1,0:T(8,128)(2,1)} async-done(((bf16[1,2,72,1152]{3,2,1,0:T(8,128)(2,1)}), bf16[1,2,1152,1152]{3,2,1,0:T(8,128)(2,1)}) %all-gather.3.cloned.1.call-update) | async-done | bytes 5308432 | tf_op jit(solution)/shard_map/all_gather | solution.py:49
  61.6 3.7 %multiply_reduce_fusion.2 = (f32[512]{0:T(512)S(1)}, f32[512,1152]{1,0:T(8,128)S(1)}) fusion(bf16[1,2,1152,1152]{3,2,1,0:T(8,128)(2,1)} %all-gather.3.cloned.1.call-done, bf16[256,1152]{0,1:T(8,128)(2,1)S(1)} %collective-permute-done.4, bf16[256,1152]{0,1:T(8,128)(2,1)S(1)} %bitcast.94), kind=kOutput, calls=%fused_computation.40 | convolution fusion | flops 1362492928 | bytes 6195200 | tf_op jit(solution)/shard_map/dot_general | solution.py:29
  68.7 3.9 %multiply_reduce_fusion.1 = (f32[1024]{0:T(1024)S(1)}, f32[1024,1152]{1,0:T(8,128)S(1)}) fusion(bf16[1024,1152]{0,1:T(8,128)(2,1)S(1)} %copy-done.3, bf16[1,2,1152,1152]{3,2,1,0:T(8,128)(2,1)S(1)} %copy-done.6), kind=kOutput, calls=%fused_computation.19 | convolution fusion | flops 2720267264 | bytes 9736192 | tf_op jit(solution)/shard_map/dot_general | solution.py:29
  72.6 4.1 %multiply_convert_fusion = bf16[1024,1024]{1,0:T(8,128)(2,1)S(1)} fusion(f32[]{:T(128)} %bitcast.8, f32[]{:T(128)} %bitcast.4, pred[1024]{0:T(1024)(128)(4,1)S(1)} %iota_compare_fusion.1, bf16[512,1152]{1,0:T(8,128)(2,1)S(1)} %collective-permute-done.5, bf16[512,1152]{1,0:T(8,128)(2,1)S(1)} %divide_convert_fusion.1, ...), kind=kOutput, calls=%fused_computation.20 | convolution fusion | flops 2435579904 | bytes 9180168 | tf_op jit(solution)/shard_map/dot_general | solution.py:29
  76.7 3.5 %fusion = (f32[1024]{0:T(1024)S(1)}, f32[1024,1152]{1,0:T(8,128)S(1)}) fusion(bf16[512,1152]{1,0:T(8,128)(2,1)S(1)} %collective-permute-done.5, bf16[512,1152]{1,0:T(8,128)(2,1)S(1)} %divide_convert_fusion.1, bf16[1024,1024]{1,0:T(8,128)(2,1)S(1)} %multiply_convert_fusion, f32[1024,1152]{1,0:T(8,128)S(1)} %get-tuple-element.30, f32[1024]{0:T(1024)S(1)} %add_sqrt_fusion, ...), kind=kOutput, calls=%fused_computation.12 | convolution fusion | flops 2426534912 | bytes 13901828 | tf_op jit(solution)/shard_map/dot_general | solution.py:29
  80.2 2.0 %fusion.3 = bf16[1024,1152]{1,0:T(8,128)(2,1)S(1)} fusion(f32[1024,1152]{1,0:T(8,128)S(1)} %get-tuple-element.32, f32[1024]{0:T(1024)S(1)} %bitcast.111, f32[1024]{0:T(1024)S(1)} %get-tuple-element.31, bf16[512,1152]{1,0:T(8,128)(2,1)S(1)} %collective-permute-done.5, bf16[512,1152]{1,0:T(8,128)(2,1)S(1)} %divide_convert_fusion.1), kind=kLoop, calls=%fused_computation.15 | loop fusion | flops 9437184 | bytes 9445376 | tf_op jit(solution)/shard_map/convert_element_type | solution.py:39
  83.1 3.1 %multiply_reduce_fusion = (f32[1024]{0:T(1024)S(1)}, f32[1024,1152]{1,0:T(8,128)S(1)}) fusion(f32[1024,1152]{1,0:T(8,128)S(1)} %get-tuple-element.30, f32[1024]{0:T(1024)S(1)} %add_sqrt_fusion, bf16[1024,1024]{1,0:T(8,128)(2,1)S(1)} %multiply_convert_fusion, bf16[512,1152]{1,0:T(8,128)(2,1)S(1)} %collective-permute-done.5, ...), kind=kOutput, calls=%fused_computation.18 | convolution fusion | flops 2425355264 | bytes 13901828 | tf_op jit(solution)/shard_map/dot_general | solution.py:29
  87.4 1.7 convolution_convert_fusion
  89.5 1.7 fusion.28
  91.2 1.8 %convolution_convert_fusion.1 = bf16[576,1152]{1,0:T(8,128)(2,1)S(1)} fusion(bf16[576,1024]{1,0:T(8,128)(2,1)S(1)} %bitcast.106, bf16[1024,1152]{1,0:T(8,128)(2,1)S(1)} %collective-permute-done.8, bf16[1024,1152]{1,0:T(8,128)(2,1)S(1)} %fusion.3), kind=kOutput, calls=%fused_computation.24 | convolution fusion | flops 1364336640 | bytes 7225344 | tf_op jit(solution)/shard_map/dot_general | solution.py:29
  95.6 1.5 collective-permute-start.11
  98.2 6.0 %collective-permute-done.10 = bf16[2,72,1152]{2,1,0:T(8,128)(2,1)S(1)} collective-permute-done((bf16[2,72,1152]{2,1,0:T(8,128)(2,1)S(1)}, bf16[2,72,1152]{2,1,0:T(8,128)(2,1)S(1)}, u32[]{:S(2)}, u32[]{:S(2)}) %collective-permute-start.10) | collective-permute-done | bytes 331808 | tf_op jit(solution)/shard_map/ppermute | solution.py:13
  104.5 7.3 %collective-permute-done.11 = bf16[2,72,1152]{2,1,0:T(8,128)(2,1)S(1)} collective-permute-done((bf16[2,72,1152]{2,1,0:T(8,128)(2,1)S(1)}, bf16[2,72,1152]{2,1,0:T(8,128)(2,1)S(1)}, u32[]{:S(2)}, u32[]{:S(2)}) %collective-permute-start.11) | collective-permute-done | bytes 331808 | tf_op jit(solution)/shard_map/ppermute | solution.py:13
  113.7 2.2 %collective-permute-start.15 = (bf16[72,1152]{1,0:T(8,128)(2,1)S(1)}, bf16[72,1152]{1,0:T(8,128)(2,1)S(1)}, u32[]{:S(2)}, u32[]{:S(2)}) collective-permute-start(bf16[72,1152]{1,0:T(8,128)(2,1)S(1)} %get-tuple-element.22), channel_id=1, source_target_pairs={{0,2},{2,4},{4,6},{6,0},{1,3},{3,5},{5,7},{7,1},{8,10},{10,12},{12... | collective-permute-start | bytes 497672 | tf_op jit(solution)/shard_map/ppermute | solution.py:13
  115.9 1.9 %collective-permute-start.16 = (bf16[72,1152]{1,0:T(8,128)(2,1)S(1)}, bf16[72,1152]{1,0:T(8,128)(2,1)S(1)}, u32[]{:S(2)}, u32[]{:S(2)}) collective-permute-start(bf16[72,1152]{1,0:T(8,128)(2,1)S(1)} %get-tuple-element.24), channel_id=1, source_target_pairs={{0,4},{2,6},{4,0},{6,2},{1,5},{3,7},{5,1},{7,3},{8,12},{10,14},{12... | collective-permute-start | bytes 497672 | tf_op jit(solution)/shard_map/ppermute | solution.py:13
  117.9 2.6 %collective-permute-done.15 = bf16[72,1152]{1,0:T(8,128)(2,1)S(1)} collective-permute-done((bf16[72,1152]{1,0:T(8,128)(2,1)S(1)}, bf16[72,1152]{1,0:T(8,128)(2,1)S(1)}, u32[]{:S(2)}, u32[]{:S(2)}) %collective-permute-start.15) | collective-permute-done | bytes 165920 | tf_op jit(solution)/shard_map/ppermute | solution.py:13
  120.5 1.4 collective-permute-done.17
  122.0 1.8 %collective-permute-done.16 = bf16[72,1152]{1,0:T(8,128)(2,1)S(1)} collective-permute-done((bf16[72,1152]{1,0:T(8,128)(2,1)S(1)}, bf16[72,1152]{1,0:T(8,128)(2,1)S(1)}, u32[]{:S(2)}, u32[]{:S(2)}) %collective-permute-start.16) | collective-permute-done | bytes 165920 | tf_op jit(solution)/shard_map/ppermute | solution.py:13
  124.0 23.8 %all_to_all.10 = bf16[16,88,128]{2,1,0:T(8,128)(2,1)S(1)} all-to-all(bf16[16,88,128]{2,1,0:T(8,128)(2,1)S(1)} %bitcast.100), channel_id=1, replica_groups=mesh['z'=8,'xh'=2,'xl'=2,'y'=4,'c'=2] {'z','xh'}, dimensions={0} | all-to-all | bytes 720896 | tf_op jit(solution)/shard_map/all_to_all | solution.py:25
  148.0 15.7 %all_to_all.11 = bf16[16,88,128]{2,1,0:T(8,128)(2,1)S(1)} all-to-all(bf16[16,88,128]{2,1,0:T(8,128)(2,1)S(1)} %broadcast_in_dim.20), channel_id=1, replica_groups=mesh['z'=8,'xh'=2,'xl'=2,'y'=4,'c'=2] {'z','xh'}, dimensions={0} | all-to-all | bytes 720896 | tf_op jit(solution)/shard_map/all_to_all | solution.py:25
  (72 shorter events, 20.0 us)
Async XLA Ops:
  6.5 55.0 %all-gather.3.cloned.1.call-start = ((), (), s32[]{:S(2)}) async-start(), calls=%async_computation.2 | async-start | bytes 5640192 | tf_op jit(solution)/shard_map/all_gather | solution.py:49
  8.6 16.4 %copy-start.5 = (f32[2]{0:T(128)S(1)}, f32[2]{0:T(128)}, u32[]{:S(2)}) copy-start(f32[2]{0:T(128)} %param.9) | copy-start | bytes 28
  8.6 15.2 %collective-permute-start.4 = (bf16[256,1152]{0,1:T(8,128)(2,1)S(1)}, bf16[256,1152]{0,1:T(8,128)(2,1)S(1)}, u32[]{:S(2)}, u32[]{:S(2)}) collective-permute-start(bf16[256,1152]{0,1:T(8,128)(2,1)S(1)} %bitcast.91), channel_id=1, source_target_pairs={{0,8},{8,0},{1,9},{9,1},{2,10},{10,2},{3,11},{11,3},{4,12},{12,4},... | collective-permute-start | bytes 1769480 | tf_op jit(solution)/shard_map/ppermute | solution.py:17
  12.3 18.0 %collective-permute-start.1 = (bf16[256,1152]{0,1:T(8,128)(2,1)}, bf16[256,1152]{0,1:T(8,128)(2,1)}, u32[]{:S(2)}, u32[]{:S(2)}) collective-permute-start(bf16[256,1152]{0,1:T(8,128)(2,1)} %bitcast), channel_id=1, source_target_pairs={{0,6},{2,0},{4,2},{6,4},{1,7},{3,1},{5,3},{7,5},{8,14},{10,8},{12,... | collective-permute-start | bytes 1769480 | tf_op jit(solution)/shard_map/ppermute | solution.py:13
  13.0 21.5 %collective-permute-start = (bf16[256,1152]{0,1:T(8,128)(2,1)}, bf16[256,1152]{0,1:T(8,128)(2,1)}, u32[]{:S(2)}, u32[]{:S(2)}) collective-permute-start(bf16[256,1152]{0,1:T(8,128)(2,1)} %bitcast), channel_id=1, source_target_pairs={{0,2},{2,4},{4,6},{6,0},{1,3},{3,5},{5,7},{7,1},{8,10},{10,12},{12... | collective-permute-start | bytes 1769480 | tf_op jit(solution)/shard_map/ppermute | solution.py:13
  24.9 25.2 %collective-permute-start.6 = (bf16[512,1152]{0,1:T(8,128)(2,1)}, bf16[512,1152]{0,1:T(8,128)(2,1)}, u32[]{:S(2)}, u32[]{:S(2)}) collective-permute-start(bf16[512,1152]{0,1:T(8,128)(2,1)} %pad_maximum_fusion.3), channel_id=1, source_target_pairs={{0,1},{1,0},{2,3},{3,2},{4,5},{5,4},{6,7},{7,6},{8,9},{9,8},{10,11... | collective-permute-start | bytes 3538952 | tf_op jit(solution)/shard_map/ppermute | solution.py:21
  31.3 18.7 %collective-permute-start.3 = (bf16[128,1152]{0,1:T(8,128)(2,1)S(1)}, bf16[128,1152]{0,1:T(8,128)(2,1)S(1)}, u32[]{:S(2)}, u32[]{:S(2)}) collective-permute-start(bf16[128,1152]{0,1:T(8,128)(2,1)S(1)} %slice.90), channel_id=1, source_target_pairs={{0,6},{2,0},{4,2},{6,4},{1,7},{3,1},{5,3},{7,5},{8,14},{10,8},{12,... | collective-permute-start | bytes 884744 | tf_op jit(solution)/shard_map/ppermute | solution.py:13
  35.4 14.5 %collective-permute-start.2 = (bf16[128,1152]{0,1:T(8,128)(2,1)S(1)}, bf16[128,1152]{0,1:T(8,128)(2,1)S(1)}, u32[]{:S(2)}, u32[]{:S(2)}) collective-permute-start(bf16[128,1152]{0,1:T(8,128)(2,1)S(1)} %slice.89), channel_id=1, source_target_pairs={{0,2},{2,4},{4,6},{6,0},{1,3},{3,5},{5,7},{7,1},{8,10},{10,12},{12... | collective-permute-start | bytes 884744 | tf_op jit(solution)/shard_map/ppermute | solution.py:13
  50.1 2.4 %copy-start.2 = (bf16[1024,1152]{0,1:T(8,128)(2,1)}, bf16[1024,1152]{0,1:T(8,128)(2,1)S(1)}, u32[]{:S(2)}) copy-start(bf16[1024,1152]{0,1:T(8,128)(2,1)S(1)} %constant_dynamic-update-slice_fusion) | copy-start | bytes 7077892
  65.3 2.5 %copy-start.6 = (bf16[1,2,1152,1152]{3,2,1,0:T(8,128)(2,1)S(1)}, bf16[1,2,1152,1152]{3,2,1,0:T(8,128)(2,1)}, u32[]{:S(2)}) copy-start(bf16[1,2,1152,1152]{3,2,1,0:T(8,128)(2,1)} %all-gather.3.cloned.1.call-done) | copy-start | bytes 15925252
  65.6 7.0 %collective-permute-start.5 = (bf16[512,1152]{1,0:T(8,128)(2,1)S(1)}, bf16[512,1152]{1,0:T(8,128)(2,1)S(1)}, u32[]{:S(2)}, u32[]{:S(2)}) collective-permute-start(bf16[512,1152]{1,0:T(8,128)(2,1)S(1)} %divide_convert_fusion.1), channel_id=1, source_target_pairs={{0,1},{1,0},{2,3},{3,2},{4,5},{5,4},{6,7},{7,6},{8,9},{9,8},{10,11... | collective-permute-start | bytes 3538952 | tf_op jit(solution)/shard_map/ppermute | solution.py:21
  65.9 2.8 %copy-start.3 = (bf16[1024,1152]{0,1:T(8,128)(2,1)S(1)}, bf16[1024,1152]{0,1:T(8,128)(2,1)}, u32[]{:S(2)}) copy-start(bf16[1024,1152]{0,1:T(8,128)(2,1)} %copy-done.2) | copy-start | bytes 7077892
  66.1 6.5 %collective-permute-start.7 = (f32[512,1]{0,1:T(1,128)S(1)}, f32[512,1]{0,1:T(1,128)S(1)}, u32[]{:S(2)}, u32[]{:S(2)}) collective-permute-start(f32[512,1]{0,1:T(1,128)S(1)} %bitcast.109), channel_id=1, source_target_pairs={{0,1},{1,0},{2,3},{3,2},{4,5},{5,4},{6,7},{7,6},{8,9},{9,8},{10,11... | collective-permute-start | bytes 6152 | tf_op jit(solution)/shard_map/ppermute | solution.py:21
  82.6 8.7 %collective-permute-start.8 = (bf16[1024,1152]{1,0:T(8,128)(2,1)S(1)}, bf16[1024,1152]{1,0:T(8,128)(2,1)S(1)}, u32[]{:S(2)}, u32[]{:S(2)}) collective-permute-start(bf16[1024,1152]{1,0:T(8,128)(2,1)S(1)} %pad_maximum_fusion.2), channel_id=1, source_target_pairs={{0,1},{1,0},{2,3},{3,2},{4,5},{5,4},{6,7},{7,6},{8,9},{9,8},{10,11... | collective-permute-start | bytes 7077896 | tf_op jit(solution)/shard_map/ppermute | solution.py:21
  87.3 2.1 %copy-start = (bf16[1,4,2,72,1024]{4,3,2,1,0:T(8,128)(2,1)S(1)}, bf16[1,4,2,72,1024]{4,3,2,1,0:T(8,128)(2,1)}, u32[]{:S(2)}) copy-start(bf16[1,4,2,72,1024]{4,3,2,1,0:T(8,128)(2,1)} %get-tuple-element.15) | copy-start | bytes 3538948
  87.3 2.1 %copy-start.1 = (bf16[1,4,2,72,1024]{4,3,2,1,0:T(8,128)(2,1)S(1)}, bf16[1,4,2,72,1024]{4,3,2,1,0:T(8,128)(2,1)}, u32[]{:S(2)}) copy-start(bf16[1,4,2,72,1024]{4,3,2,1,0:T(8,128)(2,1)} %get-tuple-element.16) | copy-start | bytes 3538948
  89.1 4.0 %collective-permute-start.9 = (bf16[576,1152]{1,0:T(8,128)(2,1)S(1)}, bf16[576,1152]{1,0:T(8,128)(2,1)S(1)}, u32[]{:S(2)}, u32[]{:S(2)}) collective-permute-start(bf16[576,1152]{1,0:T(8,128)(2,1)S(1)} %convolution_convert_fusion), channel_id=1, source_target_pairs={{0,1},{1,0},{2,3},{3,2},{4,5},{5,4},{6,7},{7,6},{8,9},{9,8},{10,11... | collective-permute-start | bytes 3981320 | tf_op jit(solution)/shard_map/ppermute | solution.py:21
  93.5 10.7 %collective-permute-start.10 = (bf16[2,72,1152]{2,1,0:T(8,128)(2,1)S(1)}, bf16[2,72,1152]{2,1,0:T(8,128)(2,1)S(1)}, u32[]{:S(2)}, u32[]{:S(2)}) collective-permute-start(bf16[2,72,1152]{2,1,0:T(8,128)(2,1)S(1)} %get-tuple-element.17), channel_id=1, source_target_pairs={{0,2},{2,4},{4,6},{6,0},{1,3},{3,5},{5,7},{7,1},{8,10},{10,12},{12... | collective-permute-start | bytes 995336 | tf_op jit(solution)/shard_map/ppermute | solution.py:13
  94.4 10.1 %collective-permute-start.12 = (bf16[2,72,1152]{2,1,0:T(8,128)(2,1)S(1)}, bf16[2,72,1152]{2,1,0:T(8,128)(2,1)S(1)}, u32[]{:S(2)}, u32[]{:S(2)}) collective-permute-start(bf16[2,72,1152]{2,1,0:T(8,128)(2,1)S(1)} %get-tuple-element.18), channel_id=1, source_target_pairs={{0,6},{2,0},{4,2},{6,4},{1,7},{3,1},{5,3},{7,5},{8,14},{10,8},{12,... | collective-permute-start | bytes 995336 | tf_op jit(solution)/shard_map/ppermute | solution.py:13
  95.6 16.3 %collective-permute-start.11 = (bf16[2,72,1152]{2,1,0:T(8,128)(2,1)S(1)}, bf16[2,72,1152]{2,1,0:T(8,128)(2,1)S(1)}, u32[]{:S(2)}, u32[]{:S(2)}) collective-permute-start(bf16[2,72,1152]{2,1,0:T(8,128)(2,1)S(1)} %get-tuple-element.19), channel_id=1, source_target_pairs={{0,4},{2,6},{4,0},{6,2},{1,5},{3,7},{5,1},{7,3},{8,12},{10,14},{12... | collective-permute-start | bytes 995336 | tf_op jit(solution)/shard_map/ppermute | solution.py:13
  97.2 16.3 %collective-permute-start.14 = (bf16[4,72,1152]{2,1,0:T(8,128)(2,1)S(1)}, bf16[4,72,1152]{2,1,0:T(8,128)(2,1)S(1)}, u32[]{:S(2)}, u32[]{:S(2)}) collective-permute-start(bf16[4,72,1152]{2,1,0:T(8,128)(2,1)S(1)} %bitcast.107), channel_id=1, source_target_pairs={{0,8},{8,0},{1,9},{9,1},{2,10},{10,2},{3,11},{11,3},{4,12},{12,4},... | collective-permute-start | bytes 1990664 | tf_op jit(solution)/shard_map/ppermute | solution.py:17
  112.0 5.8 %collective-permute-start.13 = (bf16[72,1152]{1,0:T(8,128)(2,1)S(1)}, bf16[72,1152]{1,0:T(8,128)(2,1)S(1)}, u32[]{:S(2)}, u32[]{:S(2)}) collective-permute-start(bf16[72,1152]{1,0:T(8,128)(2,1)S(1)} %slice_bitcast_fusion.12), channel_id=1, source_target_pairs={{0,8},{8,0},{1,9},{9,1},{2,10},{10,2},{3,11},{11,3},{4,12},{12,4},... | collective-permute-start | bytes 497672 | tf_op jit(solution)/shard_map/ppermute | solution.py:17
  113.7 10.2 %copy-start.4 = (bf16[1,2,72,1152]{3,2,1,0:T(8,128)(2,1)S(1)}, bf16[1,2,72,1152]{3,2,1,0:T(8,128)(2,1)}, u32[]{:S(2)}) copy-start(bf16[1,2,72,1152]{3,2,1,0:T(8,128)(2,1)} %param.8) | copy-start | bytes 995332
  113.7 6.8 %collective-permute-start.15 = (bf16[72,1152]{1,0:T(8,128)(2,1)S(1)}, bf16[72,1152]{1,0:T(8,128)(2,1)S(1)}, u32[]{:S(2)}, u32[]{:S(2)}) collective-permute-start(bf16[72,1152]{1,0:T(8,128)(2,1)S(1)} %get-tuple-element.22), channel_id=1, source_target_pairs={{0,2},{2,4},{4,6},{6,0},{1,3},{3,5},{5,7},{7,1},{8,10},{10,12},{12... | collective-permute-start | bytes 497672 | tf_op jit(solution)/shard_map/ppermute | solution.py:13
  115.9 6.0 %collective-permute-start.17 = (bf16[72,1152]{1,0:T(8,128)(2,1)S(1)}, bf16[72,1152]{1,0:T(8,128)(2,1)S(1)}, u32[]{:S(2)}, u32[]{:S(2)}) collective-permute-start(bf16[72,1152]{1,0:T(8,128)(2,1)S(1)} %get-tuple-element.23), channel_id=1, source_target_pairs={{0,6},{2,0},{4,2},{6,4},{1,7},{3,1},{5,3},{7,5},{8,14},{10,8},{12,... | collective-permute-start | bytes 497672 | tf_op jit(solution)/shard_map/ppermute | solution.py:13
  115.9 7.8 %collective-permute-start.16 = (bf16[72,1152]{1,0:T(8,128)(2,1)S(1)}, bf16[72,1152]{1,0:T(8,128)(2,1)S(1)}, u32[]{:S(2)}, u32[]{:S(2)}) collective-permute-start(bf16[72,1152]{1,0:T(8,128)(2,1)S(1)} %get-tuple-element.24), channel_id=1, source_target_pairs={{0,4},{2,6},{4,0},{6,2},{1,5},{3,7},{5,1},{7,3},{8,12},{10,14},{12... | collective-permute-start | bytes 497672 | tf_op jit(solution)/shard_map/ppermute | solution.py:13
Sparse Core Ops, SparseCore 0:
  9.2 52.3 all-gather.2
